TPU v7x, 512 devices: a whole 4x8x8 slice. The times are simulated.
512 devices in a mesh: gx: 128 (over x, z, y_hi), gy: 4 (over y_lo, core).
Axes of the slice: x: 4, y: 8 (y_hi: 4, y_lo: 2; y = y_hi * 2 + y_lo), z: 8, core: 2. Of those that a mesh axis runs over, the one named last changes fastest.
Arguments:
- positions: float32 [3, 65536], P(None, ('gx', 'gy')), may hold values from 0 to 2
- velocities: float32 [3, 65536], P(None, ('gx', 'gy')), may hold values from -6 to 6
- forces: float32 [3, 65536], P(None, ('gx', 'gy')), may hold values from -6 to 6
- species: int32 [65536], P(('gx', 'gy')), may hold values from 0 to 4
- inv_mass: float32 [5], replicated, may hold values from 0.5 to 2
- xface_list: int32 [32768], P(('gx', 'gy')), may hold values from 0 to 127
- yface_list: int32 [65536], P(('gx', 'gy')), may hold values from 0 to 191
- edge_center: int32 [131072], P(('gx', 'gy')), may hold values from 0 to 127
- edge_neighbor: int32 [131072], P(('gx', 'gy')), may hold values from 0 to 319, as said below
- edge_count: int32 [512], P(('gx', 'gy')), may hold values from 192 to 256, as said below
- migrants: int32 [4096, 8], P(('gx', 'gy')), may hold values from -1 to 127, as said below
- embed_center: float32 [5, 128], replicated, may hold values from -6 to 6
- embed_neighbor: float32 [5, 128], replicated, may hold values from -6 to 6
- radial_weight: float32 [8, 128], replicated, may hold values from -2 to 2
- tensor_one: float32 [128, 128], replicated, may hold values from -0.5 to 0.5
- mix_one: float32 [384, 128], replicated, may hold values from -0.3125 to 0.3125
- tensor_two: float32 [128, 128], replicated, may hold values from -0.5 to 0.5
- mix_two: float32 [384, 128], replicated, may hold values from -0.3125 to 0.3125
- final_weight: float32 [128, 128], replicated, may hold values from -0.5 to 0.5
- energy_out: float32 [128], replicated, may hold values from -0.5 to 0.5
Outputs:
- new_positions: float32 [3, 65536], P(None, ('gx', 'gy'))
- new_velocities: float32 [3, 65536], P(None, ('gx', 'gy'))
- new_forces: float32 [3, 65536], P(None, ('gx', 'gy'))
- arrivals: float32 [384, 12, 64], P('gx', 'gy')
Inputs may be any that keep to these rules, and one draw needn't show every extreme that they name: `edge_neighbor`: the first 192 slots of each brick name every ghost atom once. `edge_count`: some brick is full and some brick holds exactly 192. `migrants`: an atom is listed at most once per brick; live slots come first in each list, at least half of each list is live, and some list is full.
All inputs are finite; a program needn't handle non-finite values.
Results may differ from a plain program's by a relative error of at most 0.0003.
Values sent between devices are 32-bit elements; how exact they have to be, the bound alone decides.
A program may use at most 64 MiB of HBM per device.

v0:
```python
import jax
import jax.numpy as jnp
from jax import lax
from jax.sharding import PartitionSpec as P

BOX_SIDE = 2.0
CUTOFF = 2.0
TIME_STEP = 0.05
WIDTHS = tuple((0.1 * 20.0 ** (k / 7.0) for k in range(8)))


def with_halo(value, sides, width):
    for axis, dim in sides:
        size, length = (lax.axis_size(axis), value.shape[dim])
        up = [(i, (i + 1) % size) for i in range(size)]
        down = [(j, i) for i, j in up]
        last = lax.slice_in_dim(value, length - width, length, axis=dim)
        leading = lax.slice_in_dim(value, 0, width, axis=dim)
        before = lax.ppermute(last, axis, up)
        after = lax.ppermute(leading, axis, down)
        value = jnp.concatenate([before, value, after], axis=dim)
    return value


def product(left, right):
    return jnp.dot(left, right, precision=lax.Precision.HIGHEST, preferred_element_type=jnp.float32)


def harmonics(offset_vec):
    along_x, along_y, along_z = (offset_vec[0], offset_vec[1], offset_vec[2])
    constant = jnp.ones_like(along_x)
    return jnp.stack(
        [
            constant,
            along_x,
            along_y,
            along_z,
            along_x * along_y,
            along_y * along_z,
            along_z * along_x,
            0.5 * (along_x * along_x - along_y * along_y),
            (2.0 * along_z * along_z - along_x * along_x - along_y * along_y) * 0.28867513459481287,
        ],
        axis=1,
    )


def brick_energy(
    coords, ext_species, edge_center, edge_neighbor, edge_count, weights_all, owned_count
):
    (
        embed_center,
        embed_neighbor,
        radial_weight,
        tensor_one,
        mix_one,
        tensor_two,
        mix_two,
        final_weight,
        energy_out,
    ) = weights_all
    species_ids = jnp.arange(embed_center.shape[0], dtype=jnp.int32)
    offset_vec = (
        jnp.take(coords, edge_neighbor, axis=1) - jnp.take(coords, edge_center, axis=1)
    ) / CUTOFF
    squared = jnp.sum(offset_vec * offset_vec, axis=0)
    radial = jnp.exp(-squared[:, None] / jnp.asarray(WIDTHS, dtype=jnp.float32)[None, :])
    center_hot = (jnp.take(ext_species, edge_center)[:, None] == species_ids[None, :]).astype(
        jnp.float32
    )
    neighbor_hot = (jnp.take(ext_species, edge_neighbor)[:, None] == species_ids[None, :]).astype(
        jnp.float32
    )
    hidden = jax.nn.silu(
        product(radial, radial_weight)
        + product(center_hot, embed_center)
        + product(neighbor_hot, embed_neighbor)
    )
    harmonic = harmonics(offset_vec)
    live_mask = (jnp.arange(edge_center.shape[0], dtype=jnp.int32) < edge_count[0]).astype(
        jnp.float32
    )
    for tensor_w, mix_w in ((tensor_one, mix_one), (tensor_two, mix_two)):
        weight = product(hidden, tensor_w) * live_mask[:, None]
        outer_prod = harmonic[:, :, None] * weight[:, None, :]
        environment = jax.ops.segment_sum(outer_prod, edge_center, num_segments=owned_count)
        projected = jnp.take(environment, edge_center, axis=0) * harmonic[:, :, None]
        invariants = jnp.concatenate(
            [
                projected[:, 0],
                jnp.sum(projected[:, 1:4], axis=1),
                jnp.sum(projected[:, 4:9], axis=1),
            ],
            axis=1,
        )
        hidden = hidden + jax.nn.silu(product(invariants, mix_w))
    edge_energy = product(jax.nn.silu(product(hidden, final_weight)), energy_out)
    return jnp.sum(edge_energy * live_mask)


def pack_cells(fields, migrants):
    slot_count = migrants.shape[1]
    cell_list = []
    for cell_index in range(9):
        if cell_index == 4:
            cell_list.append(jnp.zeros((8 * slot_count,), jnp.float32))
            continue
        list_row = cell_index if cell_index < 4 else cell_index - 1
        slot_index = migrants[list_row]
        valid_mask = (slot_index >= 0).astype(jnp.float32)
        picked = jnp.take(fields, jnp.maximum(slot_index, 0), axis=1)
        moved = (
            jnp.zeros((8, 1), jnp.float32)
            .at[0, 0]
            .set((cell_index // 3 - 1) * BOX_SIDE)
            .at[1, 0]
            .set((cell_index % 3 - 1) * BOX_SIDE)
        )
        cell_list.append(((picked - moved) * valid_mask[None, :]).reshape(8 * slot_count))
    return jnp.stack(cell_list, axis=0).reshape(3, 3, 8 * slot_count)


def shards(
    positions,
    velocities,
    forces,
    species,
    inv_mass,
    xface_list,
    yface_list,
    edge_center,
    edge_neighbor,
    edge_count,
    migrants,
    embed_center,
    embed_neighbor,
    radial_weight,
    tensor_one,
    mix_one,
    tensor_two,
    mix_two,
    final_weight,
    energy_out,
):
    weights_all = (
        embed_center,
        embed_neighbor,
        radial_weight,
        tensor_one,
        mix_one,
        tensor_two,
        mix_two,
        final_weight,
        energy_out,
    )
    owned_count = positions.shape[1]
    xface_width = xface_list.shape[0] // 2
    yface_width = yface_list.shape[0] // 2
    inner_count = owned_count + 2 * xface_width
    species_ids = jnp.arange(inv_mass.shape[0], dtype=jnp.int32)
    species_row = species.astype(jnp.float32)[None, :]
    atom_inv = jnp.sum(
        (species[:, None] == species_ids[None, :]).astype(jnp.float32) * inv_mass[None, :], axis=1
    )[None, :]
    coords = positions
    veloc = velocities
    force_now = forces
    halfway = veloc + 0.5 * TIME_STEP * force_now * atom_inv
    coords = coords + TIME_STEP * halfway
    record = jnp.concatenate([coords, species_row], axis=0)
    row_count = record.shape[0]
    x_shift = jnp.zeros((row_count, 1), jnp.float32).at[0, 0].set(BOX_SIDE)
    y_shift = jnp.zeros((row_count, 1), jnp.float32).at[1, 0].set(BOX_SIDE)
    padded = with_halo(jnp.take(record, xface_list, axis=1), (("gx", 1),), xface_width)
    extended = jnp.concatenate(
        [record, padded[:, :xface_width] - x_shift, padded[:, 3 * xface_width :] + x_shift], axis=1
    )
    padded = with_halo(jnp.take(extended, yface_list, axis=1), (("gy", 1),), yface_width)
    complete = jnp.concatenate(
        [extended, padded[:, :yface_width] - y_shift, padded[:, 3 * yface_width :] + y_shift],
        axis=1,
    )
    ext_species = complete[3].astype(jnp.int32)

    def local_energy(ext_coords):
        return brick_energy(
            ext_coords,
            ext_species,
            edge_center,
            edge_neighbor,
            edge_count,
            weights_all,
            owned_count,
        )

    gradient = jax.grad(local_energy)(complete[:3])
    returned = with_halo(gradient[:, inner_count:], (("gy", 1),), yface_width)
    gradient_inner = (
        gradient[:, :inner_count]
        .at[:, yface_list]
        .add(jnp.concatenate([returned[:, :yface_width], returned[:, 3 * yface_width :]], axis=1))
    )
    returned = with_halo(gradient_inner[:, owned_count:], (("gx", 1),), xface_width)
    gradient_owned = (
        gradient_inner[:, :owned_count]
        .at[:, xface_list]
        .add(jnp.concatenate([returned[:, :xface_width], returned[:, 3 * xface_width :]], axis=1))
    )
    force_now = -gradient_owned
    veloc = halfway + 0.5 * TIME_STEP * force_now * atom_inv
    fields = jnp.concatenate([coords, veloc, species_row, jnp.ones_like(species_row)], axis=0)
    outgoing = pack_cells(fields, migrants)
    along_x = with_halo(outgoing, (("gx", 0),), 1)[4::-2]
    arrivals = with_halo(along_x, (("gy", 1),), 1)[:, 4::-2]
    return (coords, veloc, force_now, arrivals)


def solution(mesh):
    in_specs = (
        P(None, ("gx", "gy")),
        P(None, ("gx", "gy")),
        P(None, ("gx", "gy")),
        P(("gx", "gy")),
        P(),
        P(("gx", "gy")),
        P(("gx", "gy")),
        P(("gx", "gy")),
        P(("gx", "gy")),
        P(("gx", "gy")),
        P(("gx", "gy"), None),
        P(),
        P(),
        P(),
        P(),
        P(),
        P(),
        P(),
        P(),
        P(),
    )
    out_specs = (
        P(None, ("gx", "gy")),
        P(None, ("gx", "gy")),
        P(None, ("gx", "gy")),
        P("gx", "gy", None),
    )
    return jax.shard_map(shards, mesh=mesh, in_specs=in_specs, out_specs=out_specs, check_vma=False)
```

profile of v0, /device:TPU:1, one launch (start us, length us, event | category | flops | bytes accessed | tf_op | source)
XLA Modules:
  0.0 199.4 jit_solution(4035468448098057063)
XLA Ops:
  5.0 17.4 %collective-permute-start.1 = (f32[4,32]{1,0:T(4,128)S(1)}, f32[4,32]{1,0:T(4,128)S(1)}, u32[]{:S(2)}, u32[]{:S(2)}) collective-permute-start(f32[4,32]{1,0:T(4,128)S(1)} %get-tuple-element.313), channel_id=1, source_target_pairs={{4,0},{8,4},{12,8},{16,12},{20,16},{24,20},{28,24},{32,28},{36,32}... | collective-permute-start | bytes 1544 | tf_op jit(solution)/shard_map/ppermute | solution.py:20
  22.4 1.9 collective-permute-start
  36.5 2.9 %collective-permute-start.3 = (f32[4,64]{1,0:T(4,128)S(1)}, f32[4,64]{1,0:T(4,128)S(1)}, u32[]{:S(2)}, u32[]{:S(2)}) collective-permute-start(f32[4,64]{1,0:T(4,128)S(1)} %get-tuple-element.311), channel_id=1, source_target_pairs={{1,0},{2,1},{3,2},{0,3},{5,4},{6,5},{7,6},{4,7},{9,8},{10,9},{11,1... | collective-permute-start | bytes 3080 | tf_op jit(solution)/shard_map/ppermute | solution.py:20
  39.4 2.7 %collective-permute-start.2 = (f32[4,64]{1,0:T(4,128)S(1)}, f32[4,64]{1,0:T(4,128)S(1)}, u32[]{:S(2)}, u32[]{:S(2)}) collective-permute-start(f32[4,64]{1,0:T(4,128)S(1)} %get-tuple-element.312), channel_id=1, source_target_pairs={{0,1},{1,2},{2,3},{3,0},{4,5},{5,6},{6,7},{7,4},{8,9},{9,10},{10,1... | collective-permute-start | bytes 3080 | tf_op jit(solution)/shard_map/ppermute | solution.py:19
  43.8 1.9 gather_fusion.6
  45.8 1.9 gather_fusion.7
  52.9 8.9 %scatter_fusion = f32[128,9,128]{2,1,0:T(8,128)S(1)} fusion(f32[128,9,128]{2,1,0:T(8,128)S(1)} %broadcast.389.clone.1, s32[256]{0:T(256)S(1)} %copy-done.25, f32[256,9,128]{2,1,0:T(8,128)S(1)} %copy.197), kind=kCustom, calls=%fused_computation.18 | custom fusion | flops 294912 | bytes 3539968 | tf_op jit(solution)/shard_map/jvp()/scatter-add | solution.py:86
  65.7 2.1 %copy.199 = f32[256,9,128]{2,1,0:T(8,128)} copy(f32[256,9,128]{2,0,1:T(8,128)S(1)} %broadcast_multiply_fusion) | data formatting | bytes 2359296 | tf_op jit(solution)/shard_map/jvp()/mul | solution.py:85
  67.9 20.3 %scatter_fusion.1 = f32[128,9,128]{2,1,0:T(8,128)S(1)} fusion(f32[128,9,128]{2,1,0:T(8,128)S(1)} %broadcast.389.clone, s32[256]{0:T(256)S(1)} %copy-done.25, f32[256,9,128]{2,1,0:T(8,128)} %copy.199), kind=kCustom, calls=%fused_computation.19 | custom fusion | flops 294912 | bytes 3539968 | tf_op jit(solution)/shard_map/jvp()/scatter-add | solution.py:86
  88.2 2.4 %gather_fusion.9 = f32[256,9,128]{2,1,0:T(8,128)} fusion(f32[128,9,128]{2,1,0:T(8,128)S(1)} %scatter_fusion.1, s32[1024]{0:T(1024)S(1)} %pad_clamp_fusion.9), kind=kCustom, calls=%fused_computation.6.clone | custom fusion | bytes 2360320 | tf_op jit(solution)/shard_map/jvp(jit(_take))/gather | solution.py:87
  90.5 2.0 %broadcast_multiply_fusion.2 = f32[256,9,128]{2,0,1:T(8,128)S(1)} fusion(f32[256,9]{0,1:T(8,128)S(1)} %stack.15, f32[256,9,128]{2,1,0:T(8,128)} %gather_fusion.9, pred[256]{0:T(512)(128)(4,1)S(1)} %get-tuple-element.316), kind=kLoop, calls=%fused_computation.53 | loop fusion | flops 589824 | bytes 2368768 | tf_op jit(solution)/shard_map/jvp()/mul | solution.py:87
  95.8 2.1 %copy.201 = f32[256,9,128]{2,1,0:T(8,128)} copy(f32[256,9,128]{2,0,1:T(8,128)S(1)} %fusion.1) | data formatting | bytes 2359296 | tf_op jit(solution)/shard_map/transpose(jvp())/mul | solution.py:87
  98.0 20.4 %scatter_fusion.2 = f32[128,9,128]{2,1,0:T(8,128)S(1)} fusion(f32[128,9,128]{2,1,0:T(8,128)S(1)} %broadcast.389.clone.2, s32[256]{0:T(256)S(1)} %get-tuple-element.318, f32[256,9,128]{2,1,0:T(8,128)} %copy.201), kind=kCustom, calls=%fused_computation.20 | custom fusion | flops 294912 | bytes 3539968 | tf_op jit(solution)/shard_map/transpose(jvp(jit(_take)))/scatter-add | solution.py:87
  118.5 2.4 %gather_fusion.2 = f32[256,9,128]{2,1,0:T(8,128)} fusion(f32[128,9,128]{2,1,0:T(8,128)S(1)} %scatter_fusion.2, s32[1024]{0:T(1024)S(1)} %pad_clamp_fusion.8), kind=kCustom, calls=%fused_computation.16 | custom fusion | bytes 2360320 | tf_op jit(solution)/shard_map/transpose(jvp())/gather | solution.py:86
  120.9 2.6 %multiply_reduce_fusion.4 = (f32[256,9]{0,1:T(8,128)S(1)}, f32[256,128]{1,0:T(8,128)S(1)}) fusion(f32[256,128]{1,0:T(8,128)} %copy-done.16, f32[256,9,128]{2,1,0:T(8,128)} %gather_fusion.2, pred[256]{0:T(512)(128)(4,1)S(1)} %copy-done.41, f32[256,9]{0,1:T(8,128)S(1)} %stack.15), kind=kLoop, calls=%fused_computation.36 | loop fusion | flops 1439488 | bytes 1460480 | tf_op jit(solution)/shard_map/transpose(jvp())/reduce_sum | solution.py:85
  128.2 8.9 %scatter_fusion.3 = f32[128,9,128]{2,1,0:T(8,128)S(1)} fusion(f32[128,9,128]{2,1,0:T(8,128)S(1)} %broadcast.389, s32[256]{0:T(256)S(1)} %copy-done.28, f32[256,9,128]{2,1,0:T(8,128)S(1)} %copy.203), kind=kCustom, calls=%fused_computation.21 | custom fusion | flops 294912 | bytes 3539968 | tf_op jit(solution)/shard_map/transpose(jvp(jit(_take)))/scatter-add | solution.py:87
  144.8 4.1 %collective-permute-start.4 = (f32[3,64]{0,1:T(8,128)S(1)}, f32[3,64]{0,1:T(8,128)S(1)}, u32[]{:S(2)}, u32[]{:S(2)}) collective-permute-start(f32[3,64]{0,1:T(8,128)S(1)} %get-tuple-element.273), channel_id=1, source_target_pairs={{0,1},{1,2},{2,3},{3,0},{4,5},{5,6},{6,7},{7,4},{8,9},{9,10},{10,1... | collective-permute-start | bytes 2312 | tf_op jit(solution)/shard_map/ppermute | solution.py:19
  148.9 1.9 collective-permute-start.5
  151.0 3.2 %collective-permute-done.5 = f32[3,64]{0,1:T(8,128)S(1)} collective-permute-done((f32[3,64]{0,1:T(8,128)S(1)}, f32[3,64]{0,1:T(8,128)S(1)}, u32[]{:S(2)}, u32[]{:S(2)}) %collective-permute-start.5) | collective-permute-done | bytes 800 | tf_op jit(solution)/shard_map/ppermute | solution.py:20
  157.7 9.7 %collective-permute-start.7 = (f32[3,32]{0,1:T(8,128)S(1)}, f32[3,32]{0,1:T(8,128)S(1)}, u32[]{:S(2)}, u32[]{:S(2)}) collective-permute-start(f32[3,32]{0,1:T(8,128)S(1)} %get-tuple-element.276), channel_id=1, source_target_pairs={{4,0},{8,4},{12,8},{16,12},{20,16},{24,20},{28,24},{32,28},{36,32}... | collective-permute-start | bytes 1160 | tf_op jit(solution)/shard_map/ppermute | solution.py:20
  178.8 10.4 %collective-permute-start.9 = (f32[1,3,64]{2,1,0:T(4,128)S(1)}, f32[1,3,64]{2,1,0:T(4,128)S(1)}, u32[]{:S(2)}, u32[]{:S(2)}) collective-permute-start(f32[1,3,64]{2,1,0:T(4,128)S(1)} %maximum_bitcast_fusion.3), channel_id=1, source_target_pairs={{4,0},{8,4},{12,8},{16,12},{20,16},{24,20},{28,24},{32,28},{36,32}... | collective-permute-start | bytes 2312 | tf_op jit(solution)/shard_map/ppermute | solution.py:20
  190.0 3.9 %collective-permute-start.10 = (f32[3,1,64]{2,1,0:T(1,128)S(1)}, f32[3,1,64]{2,1,0:T(1,128)S(1)}, u32[]{:S(2)}, u32[]{:S(2)}) collective-permute-start(f32[3,1,64]{2,1,0:T(1,128)S(1)} %slice.409), channel_id=1, source_target_pairs={{0,1},{1,2},{2,3},{3,0},{4,5},{5,6},{6,7},{7,4},{8,9},{9,10},{10,1... | collective-permute-start | bytes 2312 | tf_op jit(solution)/shard_map/ppermute | solution.py:19
  193.9 1.9 collective-permute-start.11
  195.8 2.9 %collective-permute-done.11 = f32[3,1,64]{2,1,0:T(1,128)S(1)} collective-permute-done((f32[3,1,64]{2,1,0:T(1,128)S(1)}, f32[3,1,64]{2,1,0:T(1,128)S(1)}, u32[]{:S(2)}, u32[]{:S(2)}) %collective-permute-start.11) | collective-permute-done | bytes 800 | tf_op jit(solution)/shard_map/ppermute | solution.py:20
  (365 shorter events, 57.3 us)
Async XLA Ops:
  0.6 92.1 %copy-start = (f32[384,128]{1,0:T(8,128)S(1)}, f32[384,128]{1,0:T(8,128)}, u32[]{:S(2)}) copy-start(f32[384,128]{1,0:T(8,128)} %param.82) | copy-start | bytes 589828
  2.7 45.1 %copy-start.39 = (f32[1,128]{1,0:T(1,128)}, f32[1,128]{1,0:T(1,128)S(1)}, u32[]{:S(2)}) copy-start(f32[1,128]{1,0:T(1,128)S(1)} %convert_bitcast_fusion) | copy-start | bytes 1540
  4.2 166.0 %copy-start.26 = (f32[3,128]{1,0:T(4,128)}, f32[3,128]{1,0:T(4,128)S(1)}, u32[]{:S(2)}) copy-start(f32[3,128]{1,0:T(4,128)S(1)} %multiply_add_fusion.2) | copy-start | bytes 4612
  5.0 29.0 %collective-permute-start.1 = (f32[4,32]{1,0:T(4,128)S(1)}, f32[4,32]{1,0:T(4,128)S(1)}, u32[]{:S(2)}, u32[]{:S(2)}) collective-permute-start(f32[4,32]{1,0:T(4,128)S(1)} %get-tuple-element.313), channel_id=1, source_target_pairs={{4,0},{8,4},{12,8},{16,12},{20,16},{24,20},{28,24},{32,28},{36,32}... | collective-permute-start | bytes 1544 | tf_op jit(solution)/shard_map/ppermute | solution.py:20
  22.4 12.4 %collective-permute-start = (f32[4,32]{1,0:T(4,128)S(1)}, f32[4,32]{1,0:T(4,128)S(1)}, u32[]{:S(2)}, u32[]{:S(2)}) collective-permute-start(f32[4,32]{1,0:T(4,128)S(1)} %get-tuple-element.314), channel_id=1, source_target_pairs={{0,4},{4,8},{8,12},{12,16},{16,20},{20,24},{24,28},{28,32},{32,36}... | collective-permute-start | bytes 1544 | tf_op jit(solution)/shard_map/ppermute | solution.py:19
  27.6 62.9 %copy-start.33 = (pred[256]{0:T(512)(128)(4,1)}, pred[256]{0:T(512)(128)(4,1)S(1)}, u32[]{:S(2)}) copy-start(pred[256]{0:T(512)(128)(4,1)S(1)} %get-tuple-element.316) | copy-start | bytes 772
  28.3 90.2 %copy-start.29 = (s32[1024]{0:T(1024)}, s32[1024]{0:T(1024)S(1)}, u32[]{:S(2)}) copy-start(s32[1024]{0:T(1024)S(1)} %pad_clamp_fusion.8) | copy-start | bytes 12292
  36.5 5.6 %collective-permute-start.3 = (f32[4,64]{1,0:T(4,128)S(1)}, f32[4,64]{1,0:T(4,128)S(1)}, u32[]{:S(2)}, u32[]{:S(2)}) collective-permute-start(f32[4,64]{1,0:T(4,128)S(1)} %get-tuple-element.311), channel_id=1, source_target_pairs={{1,0},{2,1},{3,2},{0,3},{5,4},{6,5},{7,6},{4,7},{9,8},{10,9},{11,1... | collective-permute-start | bytes 3080 | tf_op jit(solution)/shard_map/ppermute | solution.py:20
  39.4 3.4 %collective-permute-start.2 = (f32[4,64]{1,0:T(4,128)S(1)}, f32[4,64]{1,0:T(4,128)S(1)}, u32[]{:S(2)}, u32[]{:S(2)}) collective-permute-start(f32[4,64]{1,0:T(4,128)S(1)} %get-tuple-element.312), channel_id=1, source_target_pairs={{0,1},{1,2},{2,3},{3,0},{4,5},{5,6},{6,7},{7,4},{8,9},{9,10},{10,1... | collective-permute-start | bytes 3080 | tf_op jit(solution)/shard_map/ppermute | solution.py:19
  49.6 48.4 %copy-start.27 = (s32[256]{0:T(256)}, s32[256]{0:T(256)S(1)}, u32[]{:S(2)}) copy-start(s32[256]{0:T(256)S(1)} %get-tuple-element.318) | copy-start | bytes 3076
  141.5 47.7 %copy-start.59 = (pred[8]{0:T(512)(128)(4,1)S(1)}, pred[8]{0:T(512)(128)(4,1)}, u32[]{:S(2)}) copy-start(pred[8]{0:T(512)(128)(4,1)} %get-tuple-element.301) | copy-start | bytes 28
  141.5 47.7 %copy-start.61 = (f32[8]{0:T(128)S(1)}, f32[8]{0:T(128)}, u32[]{:S(2)}) copy-start(f32[8]{0:T(128)} %get-tuple-element.287) | copy-start | bytes 100
  141.5 47.7 %copy-start.83 = (f32[8]{0:T(128)S(1)}, f32[8]{0:T(128)}, u32[]{:S(2)}) copy-start(f32[8]{0:T(128)} %constant.543.clone.1) | copy-start | bytes 100
  141.5 47.8 %copy-start.58 = (pred[8]{0:T(512)(128)(4,1)S(1)}, pred[8]{0:T(512)(128)(4,1)}, u32[]{:S(2)}) copy-start(pred[8]{0:T(512)(128)(4,1)} %get-tuple-element.299) | copy-start | bytes 28
  141.5 47.8 %copy-start.60 = (f32[8]{0:T(128)S(1)}, f32[8]{0:T(128)}, u32[]{:S(2)}) copy-start(f32[8]{0:T(128)} %get-tuple-element.288) | copy-start | bytes 100
  141.6 47.8 %copy-start.82 = (f32[8]{0:T(128)S(1)}, f32[8]{0:T(128)}, u32[]{:S(2)}) copy-start(f32[8]{0:T(128)} %constant.544.clone.1) | copy-start | bytes 100
  144.8 6.1 %collective-permute-start.4 = (f32[3,64]{0,1:T(8,128)S(1)}, f32[3,64]{0,1:T(8,128)S(1)}, u32[]{:S(2)}, u32[]{:S(2)}) collective-permute-start(f32[3,64]{0,1:T(8,128)S(1)} %get-tuple-element.273), channel_id=1, source_target_pairs={{0,1},{1,2},{2,3},{3,0},{4,5},{5,6},{6,7},{7,4},{8,9},{9,10},{10,1... | collective-permute-start | bytes 2312 | tf_op jit(solution)/shard_map/ppermute | solution.py:19
  148.9 5.2 %collective-permute-start.5 = (f32[3,64]{0,1:T(8,128)S(1)}, f32[3,64]{0,1:T(8,128)S(1)}, u32[]{:S(2)}, u32[]{:S(2)}) collective-permute-start(f32[3,64]{0,1:T(8,128)S(1)} %get-tuple-element.274), channel_id=1, source_target_pairs={{1,0},{2,1},{3,2},{0,3},{5,4},{6,5},{7,6},{4,7},{9,8},{10,9},{11,1... | collective-permute-start | bytes 2312 | tf_op jit(solution)/shard_map/ppermute | solution.py:20
  155.8 11.8 %collective-permute-start.6 = (f32[3,32]{0,1:T(8,128)S(1)}, f32[3,32]{0,1:T(8,128)S(1)}, u32[]{:S(2)}, u32[]{:S(2)}) collective-permute-start(f32[3,32]{0,1:T(8,128)S(1)} %get-tuple-element.275), channel_id=1, source_target_pairs={{0,4},{4,8},{8,12},{12,16},{16,20},{20,24},{24,28},{28,32},{32,36}... | collective-permute-start | bytes 1160 | tf_op jit(solution)/shard_map/ppermute | solution.py:19
  157.7 10.6 %collective-permute-start.7 = (f32[3,32]{0,1:T(8,128)S(1)}, f32[3,32]{0,1:T(8,128)S(1)}, u32[]{:S(2)}, u32[]{:S(2)}) collective-permute-start(f32[3,32]{0,1:T(8,128)S(1)} %get-tuple-element.276), channel_id=1, source_target_pairs={{4,0},{8,4},{12,8},{16,12},{20,16},{24,20},{28,24},{32,28},{36,32}... | collective-permute-start | bytes 1160 | tf_op jit(solution)/shard_map/ppermute | solution.py:20
  173.2 16.6 %collective-permute-start.8 = (f32[1,3,64]{2,1,0:T(4,128)S(1)}, f32[1,3,64]{2,1,0:T(4,128)S(1)}, u32[]{:S(2)}, u32[]{:S(2)}) collective-permute-start(f32[1,3,64]{2,1,0:T(4,128)S(1)} %maximum_bitcast_fusion.2), channel_id=1, source_target_pairs={{0,4},{4,8},{8,12},{12,16},{16,20},{20,24},{24,28},{28,32},{32,36}... | collective-permute-start | bytes 2312 | tf_op jit(solution)/shard_map/ppermute | solution.py:19
  178.8 11.1 %collective-permute-start.9 = (f32[1,3,64]{2,1,0:T(4,128)S(1)}, f32[1,3,64]{2,1,0:T(4,128)S(1)}, u32[]{:S(2)}, u32[]{:S(2)}) collective-permute-start(f32[1,3,64]{2,1,0:T(4,128)S(1)} %maximum_bitcast_fusion.3), channel_id=1, source_target_pairs={{4,0},{8,4},{12,8},{16,12},{20,16},{24,20},{28,24},{32,28},{36,32}... | collective-permute-start | bytes 2312 | tf_op jit(solution)/shard_map/ppermute | solution.py:20
  190.0 5.8 %collective-permute-start.10 = (f32[3,1,64]{2,1,0:T(1,128)S(1)}, f32[3,1,64]{2,1,0:T(1,128)S(1)}, u32[]{:S(2)}, u32[]{:S(2)}) collective-permute-start(f32[3,1,64]{2,1,0:T(1,128)S(1)} %slice.409), channel_id=1, source_target_pairs={{0,1},{1,2},{2,3},{3,0},{4,5},{5,6},{6,7},{7,4},{8,9},{9,10},{10,1... | collective-permute-start | bytes 2312 | tf_op jit(solution)/shard_map/ppermute | solution.py:19
  193.9 4.9 %collective-permute-start.11 = (f32[3,1,64]{2,1,0:T(1,128)S(1)}, f32[3,1,64]{2,1,0:T(1,128)S(1)}, u32[]{:S(2)}, u32[]{:S(2)}) collective-permute-start(f32[3,1,64]{2,1,0:T(1,128)S(1)} %slice.411), channel_id=1, source_target_pairs={{1,0},{2,1},{3,2},{0,3},{5,4},{6,5},{7,6},{4,7},{9,8},{10,9},{11,1... | collective-permute-start | bytes 2312 | tf_op jit(solution)/shard_map/ppermute | solution.py:20
  (80 other events, 1084.0 us)
where the time goes:
time: 201 us; the launch traced here: 199 us
  other arithmetic  90.3 us (45%)
  starting transfers between devices  60.6 us (30%)
  local copies, waits for them, and re-layouts  33.3 us (17%)
  waiting for transfers between devices  6.95 us (3%)
  matrix products  5.08 us (3%)
  between operations  3.21 us (2%)
    ppermute x6, starting transfers between devices, with_halo(): after = lax.ppermute(leading, axis, down)  44.2 us
    scatter-add x2, other arithmetic, brick_energy(): jnp.take(environment, edge_center, axis=0) * harmonic[:, :, None]  29.4 us
    scatter-add x2, other arithmetic, brick_energy(): jax.ops.segment_sum(outer_prod, edge_center, num_segments=owned_count)  29.2 us
    ppermute x6, starting transfers between devices, with_halo(): before = lax.ppermute(last, axis, up)  16.4 us
    ppermute x6, waiting for transfers between devices, with_halo(): after = lax.ppermute(leading, axis, down)  6.94 us
    dot_general x14, matrix products, product(): jnp.dot(left, right, precision=lax.Precision.HIGHEST, preferred_element_t...  5.08 us
    gather x8, local copies, waits for them, and re-layouts, pack_cells(): picked = jnp.take(fields, jnp.maximum(slot_index, 0), axis=1)  4.95 us
    unnamed x184, local copies, waits for them, and re-layouts  4.52 us
  transfers between devices with their start and end apart: 12, of which 4 were waited for; matrix products, arithmetic and copies ran while one was open for 7% of the time, Pallas kernels for 0%

commit v1 on v0

v1 whole, which is shorter than its diff:
```python
import math

import jax
import jax.numpy as jnp
from jax import lax
from jax.experimental import pallas as pl
from jax.experimental.pallas import tpu as pltpu
from jax.sharding import PartitionSpec as P

BOX_SIDE = 2.0
CUTOFF = 2.0
TIME_STEP = 0.05
WIDTHS = tuple((0.1 * 20.0 ** (k / 7.0) for k in range(8)))
Y20 = 0.28867513459481287
MESH = pl.DeviceIdType.MESH
F32 = jnp.float32
BF16 = jnp.bfloat16

MOVES = tuple((a, b) for a in (-1, 0, 1) for b in (-1, 0, 1) if (a, b) != (0, 0))


def cell(dx, dy):
    return (dx + 1) * 3 + dy + 1


def iota(shape, dim):
    return lax.broadcasted_iota(jnp.int32, shape, dim)


def halves(value):
    high = value.astype(BF16)
    low = (value - high.astype(F32)).astype(BF16)
    return high, low


def halves_f32(value):
    high = value.astype(BF16).astype(F32)
    return high, value - high


def dot(left, right, contract=(1, 0)):
    return lax.dot_general(
        left, right, (((contract[0],), (contract[1],)), ((), ())), preferred_element_type=F32
    )


def lanes_at(tile, index):
    return jnp.take_along_axis(
        tile, jnp.broadcast_to(index, tile.shape), axis=1, mode="promise_in_bounds"
    )


def sigmoid(value):
    return 0.5 + 0.5 * jnp.tanh(0.5 * value)


def row_const(values, shape):
    rows = iota(shape, 0)
    result = jnp.zeros(shape, F32)
    for index, value in enumerate(values):
        result = jnp.where(rows == index, F32(value), result)
    return result


def kernel(
    n_gx,
    n_gy,
    pos_ref,
    vel_ref,
    frc_ref,
    spec_ref,
    inv_mass_ref,
    xface_ref,
    yface_ref,
    center_ref,
    neighbor_ref,
    count_ref,
    migrants_ref,
    emb_c_ref,
    emb_n_ref,
    radial_ref,
    tensor1_ref,
    mix1_ref,
    tensor2_ref,
    mix2_ref,
    final_ref,
    eout_ref,
    new_pos_ref,
    new_vel_ref,
    new_frc_ref,
    arr_ref,
    send_x,
    send_y,
    recv_a,
    send_w,
    send_z,
    send_d,
    recv_c,
    send_m,
    recv_m,
    sems_out,
    sems_in,
):
    gx = lax.axis_index("gx")
    gy = lax.axis_index("gy")

    def place(dx, dy):
        return (lax.rem(gx + (dx + n_gx), n_gx), lax.rem(gy + (dy + n_gy), n_gy))

    def copy(phase, move, source, target):
        slot = cell(*move)
        return pltpu.make_async_remote_copy(
            src_ref=source,
            dst_ref=target.at[slot],
            send_sem=sems_out.at[phase, slot],
            recv_sem=sems_in.at[phase, slot],
            device_id=place(*move),
            device_id_type=MESH,
        )

    barrier = pltpu.get_barrier_semaphore()
    for move in MOVES:
        pl.semaphore_signal(barrier, inc=1, device_id=place(*move), device_id_type=MESH)

    lane = iota((1, 128), 1)
    rows = iota((8, 128), 0)
    low_x = (lane % 64) < 32
    low_y = lane < 64

    species = spec_ref[...].reshape(1, 128)
    inv_mass = jnp.zeros((1, 128), F32)
    for k in range(inv_mass_ref.shape[0]):
        inv_mass = jnp.where(species == k, inv_mass_ref[k], inv_mass)
    halfway = vel_ref[...] + 0.5 * TIME_STEP * frc_ref[...] * inv_mass
    coords = pos_ref[...] + TIME_STEP * halfway
    new_pos_ref[...] = coords
    species_row = species.astype(F32)
    minus = jnp.full((1, 128), -1.0, F32)
    record = jnp.concatenate([coords, species_row, minus, jnp.zeros((3, 128), F32)], axis=0)

    xface = xface_ref[...].reshape(1, 64)
    xface2 = jnp.concatenate([xface, xface], axis=1)
    yface = yface_ref[...].reshape(1, 128)
    y_owned = yface < 128
    send_x[...] = lanes_at(record, xface2)
    send_y[...] = jnp.where(
        rows == 4, yface.astype(F32), lanes_at(record, jnp.where(y_owned, yface, 0))
    )
    pl.semaphore_wait(barrier, len(MOVES))
    first = [copy(0, m, send_y if m[0] == 0 else send_x, recv_a) for m in MOVES]
    for c in first:
        c.start()

    neighbor = neighbor_ref[...].reshape(1, 256)
    center = center_ref[...].reshape(1, 256)
    live = iota((1, 256), 1) < count_ref[0]
    place_n = jnp.where(
        neighbor < 128,
        neighbor,
        jnp.where(neighbor < 192, ((neighbor - 128) ^ 32) + 128, ((neighbor - 192) ^ 64) + 256),
    )
    hot_n = (iota((384, 256), 0) == place_n).astype(F32).astype(BF16)
    hot_c = (iota((128, 256), 0) == center).astype(F32).astype(BF16)
    face_rows = jnp.concatenate([jnp.where(y_owned, yface, -1), xface2], axis=1)
    hot_f = (iota((128, 256), 0) == face_rows).astype(F32).astype(BF16)
    c_live = center.astype(F32)
    rows_e = iota((8, 256), 0)
    left_c = jnp.where(rows_e == 0, jnp.where(live, c_live, -1.0), jnp.where(rows_e == 1, 1.0, 0.0))
    right_c = jnp.where(rows_e == 0, 1.0, jnp.where(rows_e == 1, jnp.where(live, -c_live, 2.0), 0.0))
    same = dot(left_c.astype(BF16), right_c.astype(BF16), (0, 0)) == 0.0
    k0 = same.astype(F32).astype(BF16)

    def merged(tensor_ref, mix_ref):
        tensor = tensor_ref[...]
        width = tensor.shape[1]
        high, low = halves(
            jnp.concatenate(
                [
                    lax.dot_general(
                        tensor,
                        mix_ref[pl.ds(width * deg, width), :],
                        (((1,), (0,)), ((), ())),
                        precision=lax.Precision.HIGHEST,
                        preferred_element_type=F32,
                    )
                    for deg in range(3)
                ],
                axis=1,
            )
        )
        return high, low

    layers = (merged(tensor1_ref, mix1_ref), merged(tensor2_ref, mix2_ref))
    final_h, final_l = halves(final_ref[...])
    pad3 = jnp.zeros((3, 128), F32)
    table = jnp.concatenate([radial_ref[...], emb_c_ref[...], pad3, emb_n_ref[...], pad3], axis=0)
    table_h, table_l = halves_f32(table)
    table_cat = jnp.concatenate(
        [table_h, table_l, table_h[:8], jnp.zeros((8, 128), F32)], axis=0
    ).astype(BF16)
    rad_h, rad_l = table_h[:8], table_l[:8]
    rad_cat = jnp.concatenate([rad_h, rad_l], axis=0).astype(BF16)

    for c in first:
        c.wait_recv()

    def pick4(tiles):
        quarter = lane // 32
        result = tiles[3]
        for q in (2, 1, 0):
            result = jnp.where(quarter == q, tiles[q], result)
        return result

    x_shift = jnp.where(rows == 0, jnp.where(low_x, BOX_SIDE, -BOX_SIDE), 0.0)
    y_shift = jnp.where(rows == 1, jnp.where(low_y, BOX_SIDE, -BOX_SIDE), 0.0)
    ghost_x = jnp.where(low_x, recv_a[cell(-1, 0)], recv_a[cell(1, 0)]) + x_shift
    far_x = (
        pick4(
            [recv_a[cell(-1, -1)], recv_a[cell(1, -1)], recv_a[cell(-1, 1)], recv_a[cell(1, 1)]]
        )
        + x_shift
    )
    ghost_y = jnp.where(low_y, recv_a[cell(0, -1)], recv_a[cell(0, 1)])
    listed = ghost_y[4:5].astype(jnp.int32)
    via_x = listed >= 128
    far_lane = jnp.where(via_x, ((listed - 128) ^ 32) + jnp.where(low_y, 0, 64), 0)
    ghost_y = jnp.where(via_x, lanes_at(far_x, far_lane), ghost_y) + y_shift
    ghost_y = jnp.where(rows == 4, jnp.where(via_x, far_lane.astype(F32), -1.0), ghost_y)

    def edge_side(tiles, index):
        parts = []
        for half in range(2):
            at = index[:, 128 * half : 128 * half + 128]
            result = lanes_at(tiles[0], at & 127)
            for number in range(1, len(tiles)):
                result = jnp.where(
                    at >= 128 * number, lanes_at(tiles[number], at & 127), result
                )
            parts.append(result)
        return jnp.concatenate(parts, axis=1)

    near = edge_side([record, ghost_x, ghost_y], place_n)
    own = edge_side([record], center)
    hot_far = (iota((128, 256), 0) == near[4:5].astype(jnp.int32)).astype(F32).astype(BF16)

    offset = (near - own) * (1.0 / CUTOFF)
    ux, uy, uz = offset[0:1], offset[1:2], offset[2:3]
    squared = ux * ux + uy * uy + uz * uz
    tees = jnp.concatenate(
        [
            ux,
            uy,
            uz,
            ux * uy,
            uy * uz,
            uz * ux,
            0.5 * (ux * ux - uy * uy),
            (2.0 * uz * uz - ux * ux - uy * uy) * Y20,
        ],
        axis=0,
    )
    minus_inv_w = row_const([-1.0 / w for w in WIDTHS], (8, 256))
    radial = jnp.exp(squared * minus_inv_w)
    hot_sc = (rows_e == own[3:4].astype(jnp.int32)).astype(F32)
    hot_sn = (rows_e == near[3:4].astype(jnp.int32)).astype(F32)
    radial_h, radial_l = halves_f32(radial)
    features = jnp.concatenate(
        [radial_h, hot_sc, hot_sn, radial_h, hot_sc, hot_sn, radial_l, jnp.zeros((8, 256), F32)],
        axis=0,
    ).astype(BF16)
    hidden_pre = dot(features, table_cat, (0, 0))

    tees_h, tees_l = halves_f32(tees)
    tees_r = jnp.concatenate([tees_h, tees_l, tees_h, jnp.zeros((8, 256), F32)], axis=0).astype(BF16)

    def degree(mask):
        left = jnp.concatenate([tees_h, tees_h, tees_l, jnp.zeros((8, 256), F32)], axis=0)
        left = jnp.where(mask, left, 0.0).astype(BF16)
        return halves(jnp.where(same, dot(left, tees_r, (0, 0)), 0.0))

    row32 = iota((32, 256), 0) % 8
    k1_h, k1_l = degree(row32 < 3)
    k2_h, k2_l = degree(row32 >= 3)

    k_wide = jnp.concatenate([k0, k1_h, k2_h], axis=1)
    k_wide_l = jnp.concatenate([k1_l, k2_l], axis=1)
    k_tall = jnp.concatenate([k0, k1_h, k2_h], axis=0)
    k_tall_l = jnp.concatenate([k1_l, k2_l], axis=0)

    sig = sigmoid(hidden_pre)
    hidden = hidden_pre * sig
    slope0 = sig * (1.0 + hidden_pre * (1.0 - sig))
    slopes, values = [], []
    for high, low in layers:
        hid_h, hid_l = halves(hidden)
        value = dot(
            jnp.concatenate([hid_h, hid_l, hid_h], axis=1),
            jnp.concatenate([high, high, low], axis=0),
        )
        val_h, val_l = halves(value)
        values.append((val_h, val_l))
        both = dot(
            k_wide,
            jnp.concatenate(
                [
                    jnp.concatenate([val_h[:, 128 * d : 128 * d + 128], val_l[:, 128 * d : 128 * d + 128]], axis=1)
                    for d in range(3)
                ],
                axis=0,
            ),
        )
        rest = dot(k_wide_l, jnp.concatenate([val_h[:, 128:256], val_h[:, 256:384]], axis=0))
        pre = both[:, :128] + both[:, 128:] + rest
        sig = sigmoid(pre)
        hidden = hidden + pre * sig
        slopes.append(sig * (1.0 + pre * (1.0 - sig)))

    hid_h, hid_l = halves(hidden)
    pre = dot(
        jnp.concatenate([hid_h, hid_l, hid_h], axis=1),
        jnp.concatenate([final_h, final_h, final_l], axis=0),
    )
    sig = sigmoid(pre)
    back = eout_ref[...].reshape(1, 128) * (sig * (1.0 + pre * (1.0 - sig)))
    back_h, back_l = halves(back)
    grad = dot(
        jnp.concatenate([back_h, back_l, back_h], axis=1),
        jnp.concatenate([final_h, final_h, final_l], axis=1),
        (1, 1),
    )
    downs = []
    for index in (1, 0):
        high, low = layers[index]
        down_h, down_l = halves(grad * slopes[index])
        downs.append((down_h, down_l))
        both = dot(k_tall, jnp.concatenate([down_h, down_l], axis=1))
        rest = dot(k_tall_l, down_h)
        parts = [both[:256, :128] + both[:256, 128:]]
        for d in (1, 2):
            at = slice(256 * d, 256 * d + 256)
            parts.append(both[at, :128] + both[at, 128:] + rest[256 * d - 256 : 256 * d])
        dv_h, dv_l = halves(jnp.concatenate(parts, axis=1))
        grad = grad + dot(
            jnp.concatenate([dv_h, dv_l, dv_h], axis=1),
            jnp.concatenate([high, high, low], axis=1),
            (1, 1),
        )
    (d2_h, d2_l), (d1_h, d1_l) = downs
    (v1_h, v1_l), (v2_h, v2_l) = values
    outer_left = jnp.concatenate([d1_h, d2_h, d1_l, d2_l, d1_h, d2_h], axis=1)
    moved = []
    for d in (1, 2):
        at = slice(128 * d, 128 * d + 128)
        outer = dot(
            outer_left,
            jnp.concatenate(
                [v1_h[:, at], v2_h[:, at], v1_h[:, at], v2_h[:, at], v1_l[:, at], v2_l[:, at]],
                axis=1,
            ),
            (1, 1),
        )
        out_h, out_l = halves(jnp.where(same, outer, 0.0))
        pair = jnp.concatenate([tees_h, tees_l], axis=0).astype(BF16)
        high_t = tees_h.astype(BF16)
        first_part = dot(pair, out_h) + dot(pair, out_h, (1, 1))
        second_part = dot(high_t, out_l) + dot(high_t, out_l, (1, 1))
        moved.append(first_part[:8] + first_part[8:] + second_part)
    d_tees = jnp.where(rows_e < 3, moved[0], moved[1])

    g_h, g_l = halves(grad * slope0)
    d_radial = dot(rad_cat, g_h, (1, 1))
    d_radial = d_radial[:8] + d_radial[8:] + dot(rad_cat[:8], g_l, (1, 1))
    d_squared = 2.0 * jnp.sum(d_radial * radial * minus_inv_w, axis=0, keepdims=True)
    dxy, dyz, dzx = d_tees[3:4], d_tees[4:5], d_tees[5:6]
    dxx, dzz = d_tees[6:7], (2.0 * Y20) * d_tees[7:8]
    dux = d_tees[0:1] + ux * (d_squared + dxx - dzz) + uy * dxy + uz * dzx
    duy = d_tees[1:2] + uy * (d_squared - dxx - dzz) + ux * dxy + uz * dyz
    duz = d_tees[2:3] + uz * (d_squared + 2.0 * dzz) + uy * dyz + ux * dzx
    d_edge = jnp.concatenate([dux, duy, duz, jnp.zeros((5, 256), F32)], axis=0)
    d_edge = jnp.where(live, d_edge * (1.0 / CUTOFF), 0.0)
    d_edge_h, d_edge_l = halves_f32(d_edge)
    d_pair = jnp.concatenate([d_edge_h, d_edge_l], axis=0).astype(BF16)

    def spread(hot):
        result = dot(d_pair, hot, (1, 1))
        return result[:8] + result[8:]

    on_ghosts = spread(hot_n[128:])
    send_z[...] = on_ghosts[:, :128]
    send_w[...] = on_ghosts[:, 128:]
    send_d[...] = spread(hot_far)
    second = [
        copy(1, m, send_w if m[0] == 0 else send_z if m[1] == 0 else send_d, recv_c) for m in MOVES
    ]
    for c in second:
        c.start()
    on_owned = spread(hot_n[:128]) - spread(hot_c)

    slots = migrants_ref[...]
    slots = jnp.concatenate([slots] * 16, axis=1)

    for c in second:
        c.wait_recv()
    from_y = jnp.where(low_y, recv_c[cell(0, 1)], recv_c[cell(0, -1)])
    from_x = jnp.where(low_x, recv_c[cell(1, 0)], recv_c[cell(-1, 0)])
    from_far = pick4(
        [recv_c[cell(1, 1)], recv_c[cell(-1, 1)], recv_c[cell(1, -1)], recv_c[cell(-1, -1)]]
    )
    from_x = jnp.where(low_y, from_x, 0.0) + from_far
    back_h, back_l = halves_f32(jnp.concatenate([from_y, from_x], axis=1))
    back = dot(jnp.concatenate([back_h, back_l], axis=0).astype(BF16), hot_f, (1, 1))
    force = -(on_owned + back[:8] + back[8:])[:3]
    veloc = halfway + 0.5 * TIME_STEP * force * inv_mass
    new_frc_ref[...] = force
    new_vel_ref[...] = veloc

    valid = slots >= 0
    at = jnp.where(valid, slots, 0)
    fields = [coords[0:1], coords[1:2], coords[2:3], veloc[0:1], veloc[1:2], veloc[2:3], species_row]
    field = lane // 8
    out = jnp.where(field == 7, 1.0, jnp.zeros((8, 128), F32))
    for number, value in enumerate(fields):
        out = jnp.where(field == number, lanes_at(jnp.broadcast_to(value, (8, 128)), at), out)
    dx_col = row_const([BOX_SIDE * m[0] for m in MOVES], (8, 128))
    dy_col = row_const([BOX_SIDE * m[1] for m in MOVES], (8, 128))
    out = out - jnp.where(field == 0, dx_col, jnp.where(field == 1, dy_col, 0.0))
    send_m[...] = jnp.where(valid, out, 0.0)
    third = [copy(2, m, send_m, recv_m) for m in MOVES]
    for c in third:
        c.start()
    for c in third:
        c.wait_recv()
    for a in range(3):
        arr_ref[a] = jnp.concatenate(
            [
                jnp.zeros((1, 64), F32)
                if (a, b) == (1, 1)
                else recv_m[3 * a + b, MOVES.index((a - 1, b - 1)), 0:64].reshape(1, 64)
                for b in range(3)
            ],
            axis=0,
        )
    for c in first + second + third:
        c.wait_send()


def solution(mesh):
    n_gx, n_gy = mesh.shape["gx"], mesh.shape["gy"]
    vmem = pl.BlockSpec(memory_space=pltpu.VMEM)
    smem = pl.BlockSpec(memory_space=pltpu.SMEM)

    def body(*args):
        def whole(*refs):
            kernel(n_gx, n_gy, *refs)

        atoms = jax.ShapeDtypeStruct(args[0].shape, F32)
        tile = pltpu.VMEM((8, 128), F32)
        tiles = pltpu.VMEM((9, 8, 128), F32)
        return pl.pallas_call(
            whole,
            out_shape=(atoms, atoms, atoms, jax.ShapeDtypeStruct((3, 3, 64), F32)),
            in_specs=[smem if i in (4, 9) else vmem for i in range(len(args))],
            out_specs=(vmem,) * 4,
            scratch_shapes=[
                tile,
                tile,
                tiles,
                tile,
                tile,
                tile,
                tiles,
                tile,
                tiles,
                pltpu.SemaphoreType.DMA((3, 9)),
                pltpu.SemaphoreType.DMA((3, 9)),
            ],
            compiler_params=pltpu.CompilerParams(
                collective_id=0, has_side_effects=True, vmem_limit_bytes=32 * 1024 * 1024
            ),
        )(*args)

    bricks = ("gx", "gy")
    atoms_spec = P(None, bricks)
    in_specs = (
        (atoms_spec,) * 3
        + (P(bricks), P())
        + (P(bricks),) * 5
        + (P(bricks, None),)
        + (P(),) * 9
    )
    return jax.shard_map(
        body,
        mesh=mesh,
        in_specs=in_specs,
        out_specs=(atoms_spec,) * 3 + (P("gx", "gy", None),),
        check_vma=False,
    )
```

time: 201 us -> 54.5 us (0.27)
  other arithmetic: 90.3 us -> 0 us
  starting transfers between devices: 60.6 us -> 0 us
  Pallas kernels: 0 us -> 37.8 us
  local copies, waits for them, and re-layouts: 33.3 us -> 14.8 us
  waiting for transfers between devices: 6.95 us -> 0 us
  matrix products: 5.08 us -> 0 us
    scatter-add x8 -> x0, other arithmetic: 64 us -> none  [the longest x2 29.4 us: brick_energy(): jnp.take(environment, edge_center, axis=0) * harmonic[:, :, None]]
    ppermute x12 -> x0, starting transfers between devices: 60.6 us -> none  [the longest x6 44.2 us: with_halo(): after = lax.ppermute(leading, axis, down)]
    pallas_call x0 -> x1, Pallas kernels: none -> 37.8 us  [body(): pl.pallas_call(whole, out_shape=(atoms, atoms, atoms, jax.ShapeDtypeStruc...]
    gather x22 -> x0, local copies, waits for them, and re-layouts: 18.9 us -> none  [the longest x8 4.95 us: pack_cells(): picked = jnp.take(fields, jnp.maximum(slot_index, 0), axis=1)]
    unnamed x184 -> x42, local copies, waits for them, and re-layouts: 4.52 us -> 14.8 us
    ppermute x12 -> x0, waiting for transfers between devices: 6.95 us -> none  [the longest x6 6.94 us: with_halo(): after = lax.ppermute(leading, axis, down)]
    reduce_sum x9 -> x0, other arithmetic: 6.33 us -> none  [the longest x2 4.12 us: brick_energy(): outer_prod = harmonic[:, :, None] * weight[:, None, :]]
    mul x12 -> x0, local copies, waits for them, and re-layouts: 6.27 us -> none  [the longest x2 2.85 us: brick_energy(): jnp.take(environment, edge_center, axis=0) * harmonic[:, :, None]]
  transfers between devices with their start and end apart: 12 -> 0, of which waited for: 4 -> 0; matrix products, arithmetic and copies ran while one was open for 7% -> 0% of each run, Pallas kernels for 0% -> 0%
where the time goes in v1:
time: 54.5 us; the launch traced here: 53.9 us
  Pallas kernels  37.8 us (69%)
  local copies, waits for them, and re-layouts  14.8 us (27%)
  between operations  1.37 us (3%)
    pallas_call x1, Pallas kernels, body(): pl.pallas_call(whole, out_shape=(atoms, atoms, atoms, jax.ShapeDtypeStruc...  37.8 us
    unnamed x42, local copies, waits for them, and re-layouts  14.8 us

profile of v1, /device:TPU:1, one launch (start us, length us, event | category | flops | bytes accessed | tf_op | source)
XLA Modules:
  0.0 53.9 jit_solution(1996621202968941656)
XLA Ops:
  1.3 0.0 copy-done.12
  1.3 0.0 copy-done.14
  1.4 0.9 %copy-done = f32[384,128]{1,0:T(8,128)S(1)} copy-done((f32[384,128]{1,0:T(8,128)S(1)}, f32[384,128]{1,0:T(8,128)}, u32[]{:S(2)}) %copy-start) | copy-done | bytes 196632
  2.3 0.9 %copy-done.1 = f32[384,128]{1,0:T(8,128)S(1)} copy-done((f32[384,128]{1,0:T(8,128)S(1)}, f32[384,128]{1,0:T(8,128)}, u32[]{:S(2)}) %copy-start.1) | copy-done | bytes 196632
  3.2 0.8 %copy-done.2 = f32[128,128]{1,0:T(8,128)S(1)} copy-done((f32[128,128]{1,0:T(8,128)S(1)}, f32[128,128]{1,0:T(8,128)}, u32[]{:S(2)}) %copy-start.2) | copy-done | bytes 65560
  4.0 0.8 %copy-done.3 = f32[128,128]{1,0:T(8,128)S(1)} copy-done((f32[128,128]{1,0:T(8,128)S(1)}, f32[128,128]{1,0:T(8,128)}, u32[]{:S(2)}) %copy-start.3) | copy-done | bytes 65560
  4.9 0.8 %copy-done.4 = f32[128,128]{1,0:T(8,128)S(1)} copy-done((f32[128,128]{1,0:T(8,128)S(1)}, f32[128,128]{1,0:T(8,128)}, u32[]{:S(2)}) %copy-start.4) | copy-done | bytes 65560
  5.7 0.7 %copy-done.5 = s32[8,8]{1,0:T(8,128)S(1)} copy-done((s32[8,8]{1,0:T(8,128)S(1)}, s32[8,8]{1,0:T(8,128)}, u32[]{:S(2)}) %copy-start.5) | copy-done | bytes 280
  6.4 0.7 %copy-done.6 = f32[5,128]{1,0:T(8,128)S(1)} copy-done((f32[5,128]{1,0:T(8,128)S(1)}, f32[5,128]{1,0:T(8,128)}, u32[]{:S(2)}) %copy-start.6) | copy-done | bytes 2584
  7.1 0.7 %copy-done.7 = f32[5,128]{1,0:T(8,128)S(1)} copy-done((f32[5,128]{1,0:T(8,128)S(1)}, f32[5,128]{1,0:T(8,128)}, u32[]{:S(2)}) %copy-start.7) | copy-done | bytes 2584
  7.8 0.7 %copy-done.8 = f32[8,128]{1,0:T(8,128)S(1)} copy-done((f32[8,128]{1,0:T(8,128)S(1)}, f32[8,128]{1,0:T(8,128)}, u32[]{:S(2)}) %copy-start.8) | copy-done | bytes 4120
  8.5 0.7 %copy-done.9 = f32[3,128]{1,0:T(4,128)S(1)} copy-done((f32[3,128]{1,0:T(4,128)S(1)}, f32[3,128]{1,0:T(4,128)}, u32[]{:S(2)}) %copy-start.9) | copy-done | bytes 1560
  9.2 0.7 %copy-done.10 = f32[3,128]{1,0:T(4,128)S(1)} copy-done((f32[3,128]{1,0:T(4,128)S(1)}, f32[3,128]{1,0:T(4,128)}, u32[]{:S(2)}) %copy-start.10) | copy-done | bytes 1560
  9.8 0.7 %copy-done.11 = f32[3,128]{1,0:T(4,128)S(1)} copy-done((f32[3,128]{1,0:T(4,128)S(1)}, f32[3,128]{1,0:T(4,128)}, u32[]{:S(2)}) %copy-start.11) | copy-done | bytes 1560
  10.5 0.7 %copy-done.13 = s32[256]{0:T(256)S(1)} copy-done((s32[256]{0:T(256)S(1)}, s32[256]{0:T(256)}, u32[]{:S(2)}) %copy-start.13) | copy-done | bytes 1048
  11.2 0.7 %copy-done.15 = f32[5]{0:T(128)S(1)} copy-done((f32[5]{0:T(128)S(1)}, f32[5]{0:T(128)}, u32[]{:S(2)}) %copy-start.15) | copy-done | bytes 44
  11.9 0.7 %copy-done.16 = s32[64]{0:T(128)S(1)} copy-done((s32[64]{0:T(128)S(1)}, s32[64]{0:T(128)}, u32[]{:S(2)}) %copy-start.16) | copy-done | bytes 280
  12.5 0.7 %copy-done.17 = s32[128]{0:T(128)S(1)} copy-done((s32[128]{0:T(128)S(1)}, s32[128]{0:T(128)}, u32[]{:S(2)}) %copy-start.17) | copy-done | bytes 536
  13.2 0.7 %copy-done.18 = f32[128]{0:T(128)S(1)} copy-done((f32[128]{0:T(128)S(1)}, f32[128]{0:T(128)}, u32[]{:S(2)}) %copy-start.18) | copy-done | bytes 536
  13.8 37.8 %shard_map.219 = (f32[3,128]{1,0:T(4,128)S(1)}, f32[3,128]{1,0:T(4,128)S(1)}, f32[3,128]{1,0:T(4,128)S(1)}, f32[3,3,64]{2,1,0:T(4,128)S(1)}) custom-call(f32[3,128]{1,0:T(4,128)S(1)} %copy-done.9, f32[3,128]{1,0:T(4,128)S(1)} %copy-done.10, f32[3,128]{1,0:T(4,128)S(1)} %copy-done.11, s32[128]{0:T(128)S(1)} %copy-done.14, f32[5]{0:T(128)S(1)} %copy-done.15, ...), custom_call_target="tpu_custom_call" | custom-call | tf_op jit(solution)/shard_map/pallas_call | solution.py:459
  51.6 0.6 %copy.29 = f32[3,128]{1,0:T(4,128)} copy(f32[3,128]{1,0:T(4,128)S(1)} %get-tuple-element.8) | data formatting | bytes 3072
  52.2 0.6 %copy.30 = f32[3,128]{1,0:T(4,128)} copy(f32[3,128]{1,0:T(4,128)S(1)} %get-tuple-element.9) | data formatting | bytes 3072
  52.8 0.6 %copy.31 = f32[3,128]{1,0:T(4,128)} copy(f32[3,128]{1,0:T(4,128)S(1)} %get-tuple-element.10) | data formatting | bytes 3072
  53.3 0.6 %copy.32 = f32[3,3,64]{2,1,0:T(4,128)} copy(f32[3,3,64]{2,1,0:T(4,128)S(1)} %get-tuple-element.11) | data formatting | bytes 4608
  (19 shorter events, 0.0 us)
Async XLA Ops:
  0.6 0.7 %copy-start.12 = (s32[256]{0:T(256)S(1)}, s32[256]{0:T(256)}, u32[]{:S(2)}) copy-start(s32[256]{0:T(256)} %refs_7_.1) | copy-start | bytes 3076
  0.6 0.7 %copy-start.14 = (s32[128]{0:T(128)S(1)}, s32[128]{0:T(128)}, u32[]{:S(2)}) copy-start(s32[128]{0:T(128)} %refs_3_.1) | copy-start | bytes 1540
  1.3 0.9 %copy-start = (f32[384,128]{1,0:T(8,128)S(1)}, f32[384,128]{1,0:T(8,128)}, u32[]{:S(2)}) copy-start(f32[384,128]{1,0:T(8,128)} %refs_15_.1) | copy-start | bytes 589828
  2.3 0.9 %copy-start.1 = (f32[384,128]{1,0:T(8,128)S(1)}, f32[384,128]{1,0:T(8,128)}, u32[]{:S(2)}) copy-start(f32[384,128]{1,0:T(8,128)} %refs_17_.1) | copy-start | bytes 589828
  3.2 0.8 %copy-start.2 = (f32[128,128]{1,0:T(8,128)S(1)}, f32[128,128]{1,0:T(8,128)}, u32[]{:S(2)}) copy-start(f32[128,128]{1,0:T(8,128)} %refs_14_.1) | copy-start | bytes 196612
  4.0 0.8 %copy-start.3 = (f32[128,128]{1,0:T(8,128)S(1)}, f32[128,128]{1,0:T(8,128)}, u32[]{:S(2)}) copy-start(f32[128,128]{1,0:T(8,128)} %refs_16_.1) | copy-start | bytes 196612
  4.9 0.8 %copy-start.4 = (f32[128,128]{1,0:T(8,128)S(1)}, f32[128,128]{1,0:T(8,128)}, u32[]{:S(2)}) copy-start(f32[128,128]{1,0:T(8,128)} %refs_18_.1) | copy-start | bytes 196612
  5.7 0.7 %copy-start.5 = (s32[8,8]{1,0:T(8,128)S(1)}, s32[8,8]{1,0:T(8,128)}, u32[]{:S(2)}) copy-start(s32[8,8]{1,0:T(8,128)} %refs_10_.1) | copy-start | bytes 772
  6.4 0.7 %copy-start.6 = (f32[5,128]{1,0:T(8,128)S(1)}, f32[5,128]{1,0:T(8,128)}, u32[]{:S(2)}) copy-start(f32[5,128]{1,0:T(8,128)} %refs_11_.1) | copy-start | bytes 7684
  7.1 0.7 %copy-start.7 = (f32[5,128]{1,0:T(8,128)S(1)}, f32[5,128]{1,0:T(8,128)}, u32[]{:S(2)}) copy-start(f32[5,128]{1,0:T(8,128)} %refs_12_.1) | copy-start | bytes 7684
  7.8 0.7 %copy-start.8 = (f32[8,128]{1,0:T(8,128)S(1)}, f32[8,128]{1,0:T(8,128)}, u32[]{:S(2)}) copy-start(f32[8,128]{1,0:T(8,128)} %refs_13_.1) | copy-start | bytes 12292
  8.5 0.7 %copy-start.9 = (f32[3,128]{1,0:T(4,128)S(1)}, f32[3,128]{1,0:T(4,128)}, u32[]{:S(2)}) copy-start(f32[3,128]{1,0:T(4,128)} %refs_0_.1) | copy-start | bytes 4612
  9.2 0.7 %copy-start.10 = (f32[3,128]{1,0:T(4,128)S(1)}, f32[3,128]{1,0:T(4,128)}, u32[]{:S(2)}) copy-start(f32[3,128]{1,0:T(4,128)} %refs_1_.1) | copy-start | bytes 4612
  9.8 0.7 %copy-start.11 = (f32[3,128]{1,0:T(4,128)S(1)}, f32[3,128]{1,0:T(4,128)}, u32[]{:S(2)}) copy-start(f32[3,128]{1,0:T(4,128)} %refs_2_.1) | copy-start | bytes 4612
  10.5 0.7 %copy-start.13 = (s32[256]{0:T(256)S(1)}, s32[256]{0:T(256)}, u32[]{:S(2)}) copy-start(s32[256]{0:T(256)} %refs_8_.1) | copy-start | bytes 3076
  11.2 0.7 %copy-start.15 = (f32[5]{0:T(128)S(1)}, f32[5]{0:T(128)}, u32[]{:S(2)}) copy-start(f32[5]{0:T(128)} %refs_4_.1) | copy-start | bytes 64
  11.9 0.7 %copy-start.16 = (s32[64]{0:T(128)S(1)}, s32[64]{0:T(128)}, u32[]{:S(2)}) copy-start(s32[64]{0:T(128)} %refs_5_.1) | copy-start | bytes 772
  12.5 0.7 %copy-start.17 = (s32[128]{0:T(128)S(1)}, s32[128]{0:T(128)}, u32[]{:S(2)}) copy-start(s32[128]{0:T(128)} %refs_6_.1) | copy-start | bytes 1540
  13.2 0.7 %copy-start.18 = (f32[128]{0:T(128)S(1)}, f32[128]{0:T(128)}, u32[]{:S(2)}) copy-start(f32[128]{0:T(128)} %refs_19_.1) | copy-start | bytes 1540

commit v2 on v1

--- a/solution.py
+++ b/solution.py
@@ -1,5 +1,3 @@
-import math
-
 import jax
 import jax.numpy as jnp
 from jax import lax
@@ -15,8 +13,36 @@
 MESH = pl.DeviceIdType.MESH
 F32 = jnp.float32
 BF16 = jnp.bfloat16
+VMEM_BYTES = 32 * 1024 * 1024
 
 MOVES = tuple((a, b) for a in (-1, 0, 1) for b in (-1, 0, 1) if (a, b) != (0, 0))
+FAR_FIRST = tuple(sorted(MOVES, key=lambda move: -abs(move[0])))
+
+
+INPUTS = (
+    "pos",
+    "vel",
+    "frc",
+    "spec",
+    "inv_mass",
+    "xface",
+    "yface",
+    "center",
+    "neighbor",
+    "count",
+    "migrants",
+    "emb_c",
+    "emb_n",
+    "radial",
+    "tensor1",
+    "mix1",
+    "tensor2",
+    "mix2",
+    "final",
+    "eout",
+)
+FIRST = ("spec", "inv_mass", "frc", "vel", "pos", "xface", "yface")
+LOAD_ORDER = FIRST + tuple(name for name in INPUTS if name not in FIRST and name != "count")
 
 
 def cell(dx, dy):
@@ -62,56 +88,37 @@
     return result
 
 
-def kernel(
-    n_gx,
-    n_gy,
-    pos_ref,
-    vel_ref,
-    frc_ref,
-    spec_ref,
-    inv_mass_ref,
-    xface_ref,
-    yface_ref,
-    center_ref,
-    neighbor_ref,
-    count_ref,
-    migrants_ref,
-    emb_c_ref,
-    emb_n_ref,
-    radial_ref,
-    tensor1_ref,
-    mix1_ref,
-    tensor2_ref,
-    mix2_ref,
-    final_ref,
-    eout_ref,
-    new_pos_ref,
-    new_vel_ref,
-    new_frc_ref,
-    arr_ref,
-    send_x,
-    send_y,
-    recv_a,
-    send_w,
-    send_z,
-    send_d,
-    recv_c,
-    send_m,
-    recv_m,
-    sems_out,
-    sems_in,
-):
+def kernel(n_gx, n_gy, *refs):
+    count = len(INPUTS)
+    sources, refs = refs[:count], refs[count:]
+    (new_pos_ref, new_vel_ref, new_frc_ref, arr_ref), refs = refs[:4], refs[4:]
+    local, refs = refs[:count], refs[count:]
+    send_x, send_y, recv_a, send_m, recv_m, send_c, recv_c, load_sems, sems_out, sems_in = refs
+    loads = {
+        name: pltpu.make_async_copy(sources[i], local[i], load_sems.at[i])
+        for i, name in enumerate(INPUTS)
+        if name != "count"
+    }
+    refs_of = dict(zip(INPUTS, local))
+    count_ref = sources[INPUTS.index("count")]
+    for name in LOAD_ORDER:
+        loads[name].start()
+
+    def loaded(*wanted):
+        for name in wanted:
+            loads[name].wait()
+        return [refs_of[name] for name in wanted]
+
     gx = lax.axis_index("gx")
     gy = lax.axis_index("gy")
 
     def place(dx, dy):
         return (lax.rem(gx + (dx + n_gx), n_gx), lax.rem(gy + (dy + n_gy), n_gy))
 
-    def copy(phase, move, source, target):
-        slot = cell(*move)
+    def copy(phase, move, source, target, slot):
         return pltpu.make_async_remote_copy(
             src_ref=source,
-            dst_ref=target.at[slot],
+            dst_ref=target,
             send_sem=sems_out.at[phase, slot],
             recv_sem=sems_in.at[phase, slot],
             device_id=place(*move),
@@ -127,6 +134,7 @@
     low_x = (lane % 64) < 32
     low_y = lane < 64
 
+    spec_ref, inv_mass_ref, frc_ref, vel_ref, pos_ref, xface_ref, yface_ref = loaded(*FIRST)
     species = spec_ref[...].reshape(1, 128)
     inv_mass = jnp.zeros((1, 128), F32)
     for k in range(inv_mass_ref.shape[0]):
@@ -142,15 +150,47 @@
     xface2 = jnp.concatenate([xface, xface], axis=1)
     yface = yface_ref[...].reshape(1, 128)
     y_owned = yface < 128
-    send_x[...] = lanes_at(record, xface2)
-    send_y[...] = jnp.where(
-        rows == 4, yface.astype(F32), lanes_at(record, jnp.where(y_owned, yface, 0))
-    )
+    lists = jnp.concatenate(
+        [
+            jnp.zeros((4, 128), F32),
+            yface.astype(F32),
+            xface2.astype(F32),
+            jnp.where(y_owned, yface, -1).astype(F32),
+            jnp.zeros((1, 128), F32),
+        ],
+        axis=0,
+    )
+    send_x[...] = jnp.where(rows < 5, lanes_at(record, xface2), lists)
+    send_y[...] = jnp.where(rows < 4, lanes_at(record, jnp.where(y_owned, yface, 0)), lists)
     pl.semaphore_wait(barrier, len(MOVES))
-    first = [copy(0, m, send_y if m[0] == 0 else send_x, recv_a) for m in MOVES]
+    first = [
+        copy(0, m, send_y if m[0] == 0 else send_x, recv_a.at[cell(*m)], cell(*m)) for m in FAR_FIRST
+    ]
     for c in first:
         c.start()
 
+    (migrants_ref,) = loaded("migrants")
+    slots = jnp.concatenate([migrants_ref[...]] * 16, axis=1)
+    valid = slots >= 0
+    at = jnp.where(valid, slots, 0)
+    field = lane // 8
+    gain = 0.5 * TIME_STEP * inv_mass
+    out = jnp.where(field == 7, 1.0, jnp.zeros((8, 128), F32))
+    fields = [coords[0:1], coords[1:2], coords[2:3]]
+    fields += [halfway[0:1], halfway[1:2], halfway[2:3], species_row, None, gain]
+    for number, value in enumerate(fields):
+        if value is not None:
+            out = jnp.where(field == number, lanes_at(jnp.broadcast_to(value, (8, 128)), at), out)
+    dx_col = row_const([BOX_SIDE * m[0] for m in MOVES], (8, 128))
+    dy_col = row_const([BOX_SIDE * m[1] for m in MOVES], (8, 128))
+    out = out - jnp.where(field == 0, dx_col, jnp.where(field == 1, dy_col, 0.0))
+    out = jnp.where(valid, out, 0.0)
+    send_m[...] = jnp.where(field == 9, slots.astype(F32), out)
+    leave = [copy(1, m, send_m, recv_m.at[cell(*m)], cell(*m)) for m in MOVES]
+    for c in leave:
+        c.start()
+
+    neighbor_ref, center_ref = loaded("neighbor", "center")
     neighbor = neighbor_ref[...].reshape(1, 256)
     center = center_ref[...].reshape(1, 256)
     live = iota((1, 256), 1) < count_ref[0]
@@ -159,8 +199,10 @@
         neighbor,
         jnp.where(neighbor < 192, ((neighbor - 128) ^ 32) + 128, ((neighbor - 192) ^ 64) + 256),
     )
-    hot_n = (iota((384, 256), 0) == place_n).astype(F32).astype(BF16)
-    hot_c = (iota((128, 256), 0) == center).astype(F32).astype(BF16)
+    hot_n = (iota((384, 256), 0) == place_n).astype(F32)
+    hot_c = (iota((128, 256), 0) == center).astype(F32)
+    hot_owned = (hot_n[:128] - hot_c).astype(BF16)
+    hot_ghosts = hot_n[128:].astype(BF16)
     face_rows = jnp.concatenate([jnp.where(y_owned, yface, -1), xface2], axis=1)
     hot_f = (iota((128, 256), 0) == face_rows).astype(F32).astype(BF16)
     c_live = center.astype(F32)
@@ -190,6 +232,9 @@
         )
         return high, low
 
+    tensor1_ref, mix1_ref, tensor2_ref, mix2_ref = loaded("tensor1", "mix1", "tensor2", "mix2")
+    final_ref, radial_ref, emb_c_ref, emb_n_ref = loaded("final", "radial", "emb_c", "emb_n")
+    (eout_ref,) = loaded("eout")
     layers = (merged(tensor1_ref, mix1_ref), merged(tensor2_ref, mix2_ref))
     final_h, final_l = halves(final_ref[...])
     pad3 = jnp.zeros((3, 128), F32)
@@ -376,108 +421,171 @@
     dux = d_tees[0:1] + ux * (d_squared + dxx - dzz) + uy * dxy + uz * dzx
     duy = d_tees[1:2] + uy * (d_squared - dxx - dzz) + ux * dxy + uz * dyz
     duz = d_tees[2:3] + uz * (d_squared + 2.0 * dzz) + uy * dyz + ux * dzx
-    d_edge = jnp.concatenate([dux, duy, duz, jnp.zeros((5, 256), F32)], axis=0)
+    d_edge = jnp.concatenate([dux, duy, duz, dux, duy, duz, jnp.zeros((2, 256), F32)], axis=0)
     d_edge = jnp.where(live, d_edge * (1.0 / CUTOFF), 0.0)
     d_edge_h, d_edge_l = halves_f32(d_edge)
     d_pair = jnp.concatenate([d_edge_h, d_edge_l], axis=0).astype(BF16)
 
-    def spread(hot):
-        result = dot(d_pair, hot, (1, 1))
-        return result[:8] + result[8:]
-
-    on_ghosts = spread(hot_n[128:])
-    send_z[...] = on_ghosts[:, :128]
-    send_w[...] = on_ghosts[:, 128:]
-    send_d[...] = spread(hot_far)
-    second = [
-        copy(1, m, send_w if m[0] == 0 else send_z if m[1] == 0 else send_d, recv_c) for m in MOVES
-    ]
+    spread = dot(d_pair, jnp.concatenate([hot_owned, hot_ghosts, hot_far], axis=0), (1, 1))
+    spread = spread[:8] + spread[8:]
+    own_y = jnp.where(rows < 3, spread[:, :128], spread[:, 256:384])
+    far_x = jnp.where(rows < 3, spread[:, 384:], spread[:, 128:256])
+    send_c[0] = own_y
+    send_c[1] = far_x
+
+    def seat(ox, oy):
+        return (ox + 2) * n_gy + oy % n_gy
+
+    second = []
+    for mx in (-2, 2, -1, 1, 0):
+        for my in (2, -1, 1, 0):
+            if (mx, my) != (0, 0):
+                slot = seat(-mx, -my)
+                pair = (send_c, recv_c.at[slot])
+                if abs(mx) == 2:
+                    pair = (send_c.at[1], recv_c.at[slot, 1])
+                second.append(copy(2, (mx, my), *pair, slot))
     for c in second:
         c.start()
-    on_owned = spread(hot_n[:128]) - spread(hot_c)
-
-    slots = migrants_ref[...]
-    slots = jnp.concatenate([slots] * 16, axis=1)
+
+    for c in leave:
+        c.wait_recv()
+    arriving = jnp.zeros((8, 128), F32)
+    for c, m in enumerate(MOVES):
+        arriving = jnp.where(rows == c, recv_m[cell(*m)], arriving)
+    slot_lane = lane % 8
+    gains = lanes_at(arriving, 64 + slot_lane)
+    listed = lanes_at(arriving, 72 + slot_lane)
+    listed_row = jnp.sum(jnp.where(rows == field, listed, 0.0), axis=0, keepdims=True)
+    listed_at = jnp.maximum(listed_row, 0.0).astype(jnp.int32)
+    spots = iota((64, 128), 0)
+    arriving_lists = jnp.where(field == 9, arriving, 0.0).astype(BF16)
+    from_source = (iota((64, 8), 0) // 8 == iota((64, 8), 1)).astype(F32).astype(BF16)
+    listed_col = jnp.sum(
+        jnp.where(
+            iota((64, 128), 1) == 72 + spots % 8, dot(from_source, arriving_lists), 0.0
+        ),
+        axis=1,
+        keepdims=True,
+    )
+    spot_source = iota((64, 256), 0) // 8
+    hot_spots = []
+    for c, m in enumerate(MOVES):
+        tile = recv_a[cell(*m)]
+        faces = jnp.concatenate([tile[6:7], tile[5:6]], axis=1)
+        hit = jnp.where(spot_source == c, faces, -2.0) == listed_col
+        hot_spots.append(hit.astype(F32).astype(BF16))
+    hot_spots = jnp.concatenate(hot_spots, axis=1)
 
     for c in second:
         c.wait_recv()
-    from_y = jnp.where(low_y, recv_c[cell(0, 1)], recv_c[cell(0, -1)])
-    from_x = jnp.where(low_x, recv_c[cell(1, 0)], recv_c[cell(-1, 0)])
-    from_far = pick4(
-        [recv_c[cell(1, 1)], recv_c[cell(-1, 1)], recv_c[cell(1, -1)], recv_c[cell(-1, -1)]]
-    )
-    from_x = jnp.where(low_y, from_x, 0.0) + from_far
-    back_h, back_l = halves_f32(jnp.concatenate([from_y, from_x], axis=1))
-    back = dot(jnp.concatenate([back_h, back_l], axis=0).astype(BF16), hot_f, (1, 1))
-    force = -(on_owned + back[:8] + back[8:])[:3]
-    veloc = halfway + 0.5 * TIME_STEP * force * inv_mass
+
+    def part(ox, oy, tile):
+        if (ox, oy) == (0, 0):
+            return (own_y, far_x)[tile]
+        return recv_c[seat(ox, oy), tile]
+
+    def inward(bx, by):
+        from_y = jnp.where(low_y, part(bx, by - 1, 0), part(bx, by + 1, 0))
+        from_x = jnp.where(low_x, part(bx - 1, by, 1), part(bx + 1, by, 1))
+        from_far = pick4(
+            [part(bx + sx, by + sy, 1) for sx, sy in ((-1, -1), (1, -1), (-1, 1), (1, 1))]
+        )
+        both = jnp.concatenate(
+            [jnp.where(rows < 3, 0.0, from_y), jnp.where(rows < 3, from_far, from_x)], axis=1
+        )
+        return jnp.concatenate(halves_f32(both), axis=0).astype(BF16)
+
+    def force_of(owned, back):
+        back = back[:8] + back[8:]
+        return -(owned[:3] + back[:3] + back[3:6])
+
+    force = force_of(own_y, dot(inward(0, 0), hot_f, (1, 1)))
     new_frc_ref[...] = force
-    new_vel_ref[...] = veloc
-
-    valid = slots >= 0
-    at = jnp.where(valid, slots, 0)
-    fields = [coords[0:1], coords[1:2], coords[2:3], veloc[0:1], veloc[1:2], veloc[2:3], species_row]
-    field = lane // 8
-    out = jnp.where(field == 7, 1.0, jnp.zeros((8, 128), F32))
-    for number, value in enumerate(fields):
-        out = jnp.where(field == number, lanes_at(jnp.broadcast_to(value, (8, 128)), at), out)
-    dx_col = row_const([BOX_SIDE * m[0] for m in MOVES], (8, 128))
-    dy_col = row_const([BOX_SIDE * m[1] for m in MOVES], (8, 128))
-    out = out - jnp.where(field == 0, dx_col, jnp.where(field == 1, dy_col, 0.0))
-    send_m[...] = jnp.where(valid, out, 0.0)
-    third = [copy(2, m, send_m, recv_m) for m in MOVES]
-    for c in third:
-        c.start()
-    for c in third:
-        c.wait_recv()
+    new_vel_ref[...] = halfway + gain * force
+
+    owned = jnp.zeros((8, 128), F32)
+    for c, m in enumerate(MOVES):
+        owned = jnp.where(field == c, lanes_at(part(-m[0], -m[1], 0), listed_at), owned)
+    back = dot(
+        jnp.concatenate([inward(-m[0], -m[1]) for m in MOVES], axis=1), hot_spots, (1, 1)
+    )
+    back = jnp.concatenate([back, jnp.zeros((16, 64), F32)], axis=1)
+    arriving_force = force_of(owned, back)
+    push = jnp.zeros((8, 128), F32)
+    for axis in range(3):
+        value = jnp.broadcast_to(arriving_force[axis : axis + 1], (8, 128))
+        push = jnp.where(field == 3 + axis, lanes_at(value, rows * 8 + slot_lane), push)
+    result = arriving + gains * push
     for a in range(3):
         arr_ref[a] = jnp.concatenate(
             [
                 jnp.zeros((1, 64), F32)
                 if (a, b) == (1, 1)
-                else recv_m[3 * a + b, MOVES.index((a - 1, b - 1)), 0:64].reshape(1, 64)
+                else result[MOVES.index((a - 1, b - 1)), 0:64].reshape(1, 64)
                 for b in range(3)
             ],
             axis=0,
         )
-    for c in first + second + third:
+    for c in first + leave + second:
         c.wait_send()
+
+
+def store(*refs):
+    copies = [pltpu.make_async_copy(refs[i], refs[4 + i], refs[8].at[i]) for i in range(4)]
+    for c in copies:
+        c.start()
+    for c in copies:
+        c.wait()
 
 
 def solution(mesh):
     n_gx, n_gy = mesh.shape["gx"], mesh.shape["gy"]
     vmem = pl.BlockSpec(memory_space=pltpu.VMEM)
     smem = pl.BlockSpec(memory_space=pltpu.SMEM)
+    hbm = pl.BlockSpec(memory_space=pltpu.HBM)
+
+    def hold(name, arg):
+        return arg if name == "count" else pltpu.with_memory_space_constraint(arg, pltpu.HBM)
 
     def body(*args):
         def whole(*refs):
             kernel(n_gx, n_gy, *refs)
 
         atoms = jax.ShapeDtypeStruct(args[0].shape, F32)
+        outs = (atoms, atoms, atoms, jax.ShapeDtypeStruct((3, 3, 64), F32))
         tile = pltpu.VMEM((8, 128), F32)
         tiles = pltpu.VMEM((9, 8, 128), F32)
-        return pl.pallas_call(
+        scalars = ("inv_mass", "count")
+        results = pl.pallas_call(
             whole,
-            out_shape=(atoms, atoms, atoms, jax.ShapeDtypeStruct((3, 3, 64), F32)),
-            in_specs=[smem if i in (4, 9) else vmem for i in range(len(args))],
+            out_shape=outs,
+            in_specs=[smem if name == "count" else hbm for name in INPUTS],
             out_specs=(vmem,) * 4,
             scratch_shapes=[
-                tile,
-                tile,
-                tiles,
-                tile,
-                tile,
-                tile,
-                tiles,
-                tile,
-                tiles,
-                pltpu.SemaphoreType.DMA((3, 9)),
-                pltpu.SemaphoreType.DMA((3, 9)),
+                (pltpu.SMEM if name in scalars else pltpu.VMEM)(arg.shape, arg.dtype)
+                for name, arg in zip(INPUTS, args)
+            ]
+            + [tile, tile, tiles, tile, tiles]
+            + [
+                pltpu.VMEM((2, 8, 128), F32),
+                pltpu.VMEM((5 * n_gy, 2, 8, 128), F32),
+                pltpu.SemaphoreType.DMA((len(args),)),
+                pltpu.SemaphoreType.DMA((3, 5 * n_gy)),
+                pltpu.SemaphoreType.DMA((3, 5 * n_gy)),
             ],
             compiler_params=pltpu.CompilerParams(
-                collective_id=0, has_side_effects=True, vmem_limit_bytes=32 * 1024 * 1024
+                collective_id=0, has_side_effects=True, vmem_limit_bytes=VMEM_BYTES
             ),
-        )(*args)
+        )(*(hold(name, arg) for name, arg in zip(INPUTS, args)))
+        return pl.pallas_call(
+            store,
+            out_shape=outs,
+            in_specs=[vmem] * 4,
+            out_specs=(hbm,) * 4,
+            scratch_shapes=[pltpu.SemaphoreType.DMA((4,))],
+            compiler_params=pltpu.CompilerParams(vmem_limit_bytes=VMEM_BYTES),
+        )(*results)
 
     bricks = ("gx", "gy")
     atoms_spec = P(None, bricks)

time: 54.5 us -> 36.7 us (0.67)
  local copies, waits for them, and re-layouts: 14.8 us -> 0 us
  Pallas kernels: 37.8 us -> 35.2 us
    unnamed x42 -> x0, local copies, waits for them, and re-layouts: 14.8 us -> none
    pallas_call x1 -> x2, Pallas kernels: 37.8 us -> 35.2 us  [the longest x1 34.6 us: body(): pl.pallas_call(whole, out_shape=outs, in_specs=[smem if name == 'count' e...]
where the time goes in v2:
time: 36.7 us; the launch traced here: 36.5 us
  Pallas kernels  35.2 us (96%)
  between operations  1.29 us (4%)
    pallas_call x1, Pallas kernels, body(): pl.pallas_call(whole, out_shape=outs, in_specs=[smem if name == 'count' e...  34.6 us

profile of v2, /device:TPU:1, one launch (start us, length us, event | category | flops | bytes accessed | tf_op | source)
XLA Modules:
  0.0 36.5 jit_solution(8890777090699777463)
XLA Ops:
  1.3 34.6 %shard_map.219 = (f32[3,128]{1,0:T(4,128)S(1)}, f32[3,128]{1,0:T(4,128)S(1)}, f32[3,128]{1,0:T(4,128)S(1)}, f32[3,3,64]{2,1,0:T(4,128)S(1)}) custom-call(f32[3,128]{1,0:T(4,128)} %refs_0_.1, f32[3,128]{1,0:T(4,128)} %refs_1_.1, f32[3,128]{1,0:T(4,128)} %refs_2_.1, s32[128]{0:T(128)} %refs_3_.1, f32[5]{0:T(128)} %refs_4_.1, s32[64]{0:T(128)} %refs_5_.1, ...), custom_call_target="tpu_custom_call" | custom-call | tf_op jit(solution)/shard_map/pallas_call | solution.py:560
  35.9 0.6 %shard_map.220 = (f32[3,128]{1,0:T(4,128)}, f32[3,128]{1,0:T(4,128)}, f32[3,128]{1,0:T(4,128)}, f32[3,3,64]{2,1,0:T(4,128)}) custom-call(f32[3,128]{1,0:T(4,128)S(1)} %get-tuple-element.8.refs_0_, f32[3,128]{1,0:T(4,128)S(1)} %get-tuple-element.9.refs_1_, f32[3,128]{1,0:T(4,128)S(1)} %get-tuple-element.10.refs_2_, f32[3,3,64]{2,1,0:T(4,128)S(1)} %get-tuple-element.11.refs_3_), custom_call_target="tpu_custom_call" | custom-call | tf_op jit(solution)/shard_map/pallas_call | solution.py:581

commit v3 on v2

--- a/solution.py
+++ b/solution.py
@@ -16,6 +16,8 @@
 VMEM_BYTES = 32 * 1024 * 1024
 
 MOVES = tuple((a, b) for a in (-1, 0, 1) for b in (-1, 0, 1) if (a, b) != (0, 0))
+ROW = 32
+RELAY = 3
 FAR_FIRST = tuple(sorted(MOVES, key=lambda move: -abs(move[0])))
 
 
@@ -93,7 +95,35 @@
     sources, refs = refs[:count], refs[count:]
     (new_pos_ref, new_vel_ref, new_frc_ref, arr_ref), refs = refs[:4], refs[4:]
     local, refs = refs[:count], refs[count:]
-    send_x, send_y, recv_a, send_m, recv_m, send_c, recv_c, load_sems, sems_out, sems_in = refs
+    send_x, send_y, recv_a, send_m, recv_m, send_c, recv_c, load_sems, sems_out, sems_in = refs[:10]
+    relay_sem, known_sem = refs[10:]
+    gx = lax.axis_index("gx")
+    gy = lax.axis_index("gy")
+    row = lax.rem(gx, ROW)
+
+    def place(dx, dy):
+        return (lax.rem(gx + (dx + n_gx), n_gx), lax.rem(gy + (dy + n_gy), n_gy))
+
+    def signal(semaphore, target):
+        pl.semaphore_signal(semaphore, inc=1, device_id=target, device_id_type=MESH)
+
+    barrier = pltpu.get_barrier_semaphore()
+
+    @pl.when(row == RELAY)
+    def _():
+        signal(barrier, place(ROW - 1 - RELAY, 0))
+        for dy in (-1, 0, 1):
+            signal(barrier, place(ROW - RELAY, dy))
+
+    @pl.when(row < ROW - 1)
+    def _():
+        for dy in (-1, 0, 1):
+            signal(barrier, place(1, dy))
+
+    for move in FAR_FIRST:
+        if move[0] != 1:
+            signal(barrier, place(*move))
+
     loads = {
         name: pltpu.make_async_copy(sources[i], local[i], load_sems.at[i])
         for i, name in enumerate(INPUTS)
@@ -109,25 +139,15 @@
             loads[name].wait()
         return [refs_of[name] for name in wanted]
 
-    gx = lax.axis_index("gx")
-    gy = lax.axis_index("gy")
-
-    def place(dx, dy):
-        return (lax.rem(gx + (dx + n_gx), n_gx), lax.rem(gy + (dy + n_gy), n_gy))
-
-    def copy(phase, move, source, target, slot):
+    def copy(phase, source, target, out_slot, in_slot, device):
         return pltpu.make_async_remote_copy(
             src_ref=source,
             dst_ref=target,
-            send_sem=sems_out.at[phase, slot],
-            recv_sem=sems_in.at[phase, slot],
-            device_id=place(*move),
+            send_sem=sems_out.at[phase, out_slot],
+            recv_sem=sems_in.at[phase, in_slot],
+            device_id=device,
             device_id_type=MESH,
         )
-
-    barrier = pltpu.get_barrier_semaphore()
-    for move in MOVES:
-        pl.semaphore_signal(barrier, inc=1, device_id=place(*move), device_id_type=MESH)
 
     lane = iota((1, 128), 1)
     rows = iota((8, 128), 0)
@@ -162,12 +182,32 @@
     )
     send_x[...] = jnp.where(rows < 5, lanes_at(record, xface2), lists)
     send_y[...] = jnp.where(rows < 4, lanes_at(record, jnp.where(y_owned, yface, 0)), lists)
-    pl.semaphore_wait(barrier, len(MOVES))
-    first = [
-        copy(0, m, send_y if m[0] == 0 else send_x, recv_a.at[cell(*m)], cell(*m)) for m in FAR_FIRST
-    ]
+    pl.semaphore_wait(barrier, len(MOVES) + row // (ROW - 1))
+
+    @pl.when(row == ROW - 1)
+    def _():
+        signal(relay_sem, place(RELAY + 1 - ROW, 0))
+
+    at_start = 1 - (row + (ROW - 1)) // ROW
+    first, first_in = [], []
+    for m in FAR_FIRST:
+        source, slot = send_y if m[0] == 0 else send_x, cell(*m)
+        first_in.append(copy(0, source, recv_a.at[slot], slot, slot, place(*m)))
+        if m[0] == -1:
+            there = slot + at_start * (10 + m[1] - slot)
+            target = place(-1 - at_start * (ROW - 1 - RELAY), m[1])
+            first.append(copy(0, source, recv_a.at[there], slot, there, target))
+        else:
+            first.append(first_in[-1])
     for c in first:
         c.start()
+
+    relays, relays_in = [], []
+    for dy in (-1, 0, 1):
+        here, there = 10 + dy, cell(-1, dy)
+        last = place(ROW - 1 - RELAY, 0)
+        relays_in.append(copy(0, send_x, recv_a.at[here], here, here, last))
+        relays.append(copy(0, recv_a.at[here], recv_a.at[there], here, there, last))
 
     (migrants_ref,) = loaded("migrants")
     slots = jnp.concatenate([migrants_ref[...]] * 16, axis=1)
@@ -186,9 +226,12 @@
     out = out - jnp.where(field == 0, dx_col, jnp.where(field == 1, dy_col, 0.0))
     out = jnp.where(valid, out, 0.0)
     send_m[...] = jnp.where(field == 9, slots.astype(F32), out)
-    leave = [copy(1, m, send_m, recv_m.at[cell(*m)], cell(*m)) for m in MOVES]
-    for c in leave:
-        c.start()
+    leave = [copy(1, send_m, recv_m.at[cell(*m)], cell(*m), cell(*m), place(*m)) for m in MOVES]
+    for m, c in zip(MOVES, leave):
+        if m[0] == -1:
+            pl.when(row > 0)(c.start)
+        else:
+            c.start()
 
     neighbor_ref, center_ref = loaded("neighbor", "center")
     neighbor = neighbor_ref[...].reshape(1, 256)
@@ -246,8 +289,24 @@
     rad_h, rad_l = table_h[:8], table_l[:8]
     rad_cat = jnp.concatenate([rad_h, rad_l], axis=0).astype(BF16)
 
-    for c in first:
+    @pl.when(row == RELAY)
+    def _():
+        for c in relays_in:
+            c.wait_recv()
+        pl.semaphore_wait(relay_sem, 1)
+        for c in relays:
+            c.start()
+
+    for c in first_in:
         c.wait_recv()
+
+    @pl.when(row == 0)
+    def _():
+        signal(known_sem, place(1, 0))
+        signal(known_sem, place(1, 1))
+        for m, c in zip(MOVES, leave):
+            if m[0] == -1:
+                c.start()
 
     def pick4(tiles):
         quarter = lane // 32
@@ -444,9 +503,18 @@
                 pair = (send_c, recv_c.at[slot])
                 if abs(mx) == 2:
                     pair = (send_c.at[1], recv_c.at[slot, 1])
-                second.append(copy(2, (mx, my), *pair, slot))
-    for c in second:
-        c.start()
+                c = copy(2, *pair, slot, slot, place(mx, my))
+                second.append(c)
+                if mx == -2:
+                    pl.when(row != 1)(c.start)
+                else:
+                    c.start()
+
+    @pl.when(row == 1)
+    def _():
+        pl.semaphore_wait(known_sem, 2)
+        for c in second[:n_gy]:
+            c.start()
 
     for c in leave:
         c.wait_recv()
@@ -530,6 +598,11 @@
     for c in first + leave + second:
         c.wait_send()
 
+    @pl.when(row == RELAY)
+    def _():
+        for c in relays:
+            c.wait_send()
+
 
 def store(*refs):
     copies = [pltpu.make_async_copy(refs[i], refs[4 + i], refs[8].at[i]) for i in range(4)]
@@ -566,13 +639,15 @@
                 (pltpu.SMEM if name in scalars else pltpu.VMEM)(arg.shape, arg.dtype)
                 for name, arg in zip(INPUTS, args)
             ]
-            + [tile, tile, tiles, tile, tiles]
+            + [tile, tile, pltpu.VMEM((12, 8, 128), F32), tile, tiles]
             + [
                 pltpu.VMEM((2, 8, 128), F32),
                 pltpu.VMEM((5 * n_gy, 2, 8, 128), F32),
                 pltpu.SemaphoreType.DMA((len(args),)),
                 pltpu.SemaphoreType.DMA((3, 5 * n_gy)),
                 pltpu.SemaphoreType.DMA((3, 5 * n_gy)),
+                pltpu.SemaphoreType.REGULAR,
+                pltpu.SemaphoreType.REGULAR,
             ],
             compiler_params=pltpu.CompilerParams(
                 collective_id=0, has_side_effects=True, vmem_limit_bytes=VMEM_BYTES

time: 36.7 us -> 34.4 us (0.937)
  Pallas kernels: 35.2 us -> 33 us
    pallas_call x1, Pallas kernels: 34.6 us -> 32.3 us  [body(): pl.pallas_call(whole, out_shape=outs, in_specs=[smem if name == 'count' e...]
where the time goes in v3:
time: 34.4 us; the launch traced here: 34.3 us
  Pallas kernels  33 us (96%)
  between operations  1.29 us (4%)
    pallas_call x1, Pallas kernels, body(): pl.pallas_call(whole, out_shape=outs, in_specs=[smem if name == 'count' e...  32.3 us

profile of v3, /device:TPU:1, one launch (start us, length us, event | category | flops | bytes accessed | tf_op | source)
XLA Modules:
  0.0 34.3 jit_solution(9519591473259324090)
XLA Ops:
  1.3 32.3 %shard_map.219 = (f32[3,128]{1,0:T(4,128)S(1)}, f32[3,128]{1,0:T(4,128)S(1)}, f32[3,128]{1,0:T(4,128)S(1)}, f32[3,3,64]{2,1,0:T(4,128)S(1)}) custom-call(f32[3,128]{1,0:T(4,128)} %refs_0_.1, f32[3,128]{1,0:T(4,128)} %refs_1_.1, f32[3,128]{1,0:T(4,128)} %refs_2_.1, s32[128]{0:T(128)} %refs_3_.1, f32[5]{0:T(128)} %refs_4_.1, s32[64]{0:T(128)} %refs_5_.1, ...), custom_call_target="tpu_custom_call" | custom-call | tf_op jit(solution)/shard_map/pallas_call | solution.py:633
  33.6 0.6 %shard_map.220 = (f32[3,128]{1,0:T(4,128)}, f32[3,128]{1,0:T(4,128)}, f32[3,128]{1,0:T(4,128)}, f32[3,3,64]{2,1,0:T(4,128)}) custom-call(f32[3,128]{1,0:T(4,128)S(1)} %get-tuple-element.8.refs_0_, f32[3,128]{1,0:T(4,128)S(1)} %get-tuple-element.9.refs_1_, f32[3,128]{1,0:T(4,128)S(1)} %get-tuple-element.10.refs_2_, f32[3,3,64]{2,1,0:T(4,128)S(1)} %get-tuple-element.11.refs_3_), custom_call_target="tpu_custom_call" | custom-call | tf_op jit(solution)/shard_map/pallas_call | solution.py:656

commit v4 on v3

--- a/solution.py
+++ b/solution.py
@@ -66,6 +66,13 @@
     return high, value - high
 
 
+def doubled(high, low):
+    return (
+        jnp.concatenate([jnp.concatenate([high, low], axis=1)] * 2, axis=0),
+        jnp.concatenate([jnp.concatenate([high] * 2, axis=1), jnp.concatenate([low] * 2, axis=1)], axis=0),
+    )
+
+
 def dot(left, right, contract=(1, 0)):
     return lax.dot_general(
         left, right, (((contract[0],), (contract[1],)), ((), ())), preferred_element_type=F32
@@ -139,15 +146,19 @@
             loads[name].wait()
         return [refs_of[name] for name in wanted]
 
-    def copy(phase, source, target, out_slot, in_slot, device):
+    def copy(phase, source, target, device, arrive=None):
         return pltpu.make_async_remote_copy(
             src_ref=source,
             dst_ref=target,
-            send_sem=sems_out.at[phase, out_slot],
-            recv_sem=sems_in.at[phase, in_slot],
+            send_sem=sems_out.at[phase],
+            recv_sem=sems_in.at[phase if arrive is None else arrive],
             device_id=device,
             device_id_type=MESH,
         )
+
+    def all_of(phase, ref, tiles):
+        whole = ref.at[pl.ds(0, tiles)]
+        return copy(phase, whole, whole, place(1, 0))
 
     lane = iota((1, 128), 1)
     rows = iota((8, 128), 0)
@@ -189,25 +200,15 @@
         signal(relay_sem, place(RELAY + 1 - ROW, 0))
 
     at_start = 1 - (row + (ROW - 1)) // ROW
-    first, first_in = [], []
+    last = place(ROW - 1 - RELAY, 0)
     for m in FAR_FIRST:
         source, slot = send_y if m[0] == 0 else send_x, cell(*m)
-        first_in.append(copy(0, source, recv_a.at[slot], slot, slot, place(*m)))
         if m[0] == -1:
             there = slot + at_start * (10 + m[1] - slot)
             target = place(-1 - at_start * (ROW - 1 - RELAY), m[1])
-            first.append(copy(0, source, recv_a.at[there], slot, there, target))
+            copy(0, source, recv_a.at[there], target, 3 * at_start).start()
         else:
-            first.append(first_in[-1])
-    for c in first:
-        c.start()
-
-    relays, relays_in = [], []
-    for dy in (-1, 0, 1):
-        here, there = 10 + dy, cell(-1, dy)
-        last = place(ROW - 1 - RELAY, 0)
-        relays_in.append(copy(0, send_x, recv_a.at[here], here, here, last))
-        relays.append(copy(0, recv_a.at[here], recv_a.at[there], here, there, last))
+            copy(0, source, recv_a.at[slot], place(*m)).start()
 
     (migrants_ref,) = loaded("migrants")
     slots = jnp.concatenate([migrants_ref[...]] * 16, axis=1)
@@ -226,7 +227,7 @@
     out = out - jnp.where(field == 0, dx_col, jnp.where(field == 1, dy_col, 0.0))
     out = jnp.where(valid, out, 0.0)
     send_m[...] = jnp.where(field == 9, slots.astype(F32), out)
-    leave = [copy(1, send_m, recv_m.at[cell(*m)], cell(*m), cell(*m), place(*m)) for m in MOVES]
+    leave = [copy(1, send_m, recv_m.at[cell(*m)], place(*m)) for m in MOVES]
     for m, c in zip(MOVES, leave):
         if m[0] == -1:
             pl.when(row > 0)(c.start)
@@ -273,13 +274,13 @@
                 axis=1,
             )
         )
-        return high, low
+        return doubled(high, low)
 
     tensor1_ref, mix1_ref, tensor2_ref, mix2_ref = loaded("tensor1", "mix1", "tensor2", "mix2")
     final_ref, radial_ref, emb_c_ref, emb_n_ref = loaded("final", "radial", "emb_c", "emb_n")
     (eout_ref,) = loaded("eout")
     layers = (merged(tensor1_ref, mix1_ref), merged(tensor2_ref, mix2_ref))
-    final_h, final_l = halves(final_ref[...])
+    final_forward, final_backward = doubled(*halves(final_ref[...]))
     pad3 = jnp.zeros((3, 128), F32)
     table = jnp.concatenate([radial_ref[...], emb_c_ref[...], pad3, emb_n_ref[...], pad3], axis=0)
     table_h, table_l = halves_f32(table)
@@ -291,14 +292,12 @@
 
     @pl.when(row == RELAY)
     def _():
-        for c in relays_in:
-            c.wait_recv()
+        all_of(3, recv_a, 3).wait_recv()
         pl.semaphore_wait(relay_sem, 1)
-        for c in relays:
-            c.start()
-
-    for c in first_in:
-        c.wait_recv()
+        for dy in (-1, 0, 1):
+            copy(3, recv_a.at[10 + dy], recv_a.at[cell(-1, dy)], last, 0).start()
+
+    all_of(0, recv_a, 8).wait_recv()
 
     @pl.when(row == 0)
     def _():
@@ -395,12 +394,10 @@
     hidden = hidden_pre * sig
     slope0 = sig * (1.0 + hidden_pre * (1.0 - sig))
     slopes, values = [], []
-    for high, low in layers:
+    for forward, _ in layers:
         hid_h, hid_l = halves(hidden)
-        value = dot(
-            jnp.concatenate([hid_h, hid_l, hid_h], axis=1),
-            jnp.concatenate([high, high, low], axis=0),
-        )
+        pair = dot(jnp.concatenate([hid_h, hid_l], axis=1), forward)
+        value = pair[:, :384] + pair[:, 384:]
         val_h, val_l = halves(value)
         values.append((val_h, val_l))
         both = dot(
@@ -420,21 +417,16 @@
         slopes.append(sig * (1.0 + pre * (1.0 - sig)))
 
     hid_h, hid_l = halves(hidden)
-    pre = dot(
-        jnp.concatenate([hid_h, hid_l, hid_h], axis=1),
-        jnp.concatenate([final_h, final_h, final_l], axis=0),
-    )
+    pre = dot(jnp.concatenate([hid_h, hid_l], axis=1), final_forward)
+    pre = pre[:, :128] + pre[:, 128:]
     sig = sigmoid(pre)
     back = eout_ref[...].reshape(1, 128) * (sig * (1.0 + pre * (1.0 - sig)))
     back_h, back_l = halves(back)
-    grad = dot(
-        jnp.concatenate([back_h, back_l, back_h], axis=1),
-        jnp.concatenate([final_h, final_h, final_l], axis=1),
-        (1, 1),
-    )
+    grad = dot(jnp.concatenate([back_h, back_l], axis=1), final_backward, (1, 1))
+    grad = grad[:, :128] + grad[:, 128:]
     downs = []
     for index in (1, 0):
-        high, low = layers[index]
+        _, backward = layers[index]
         down_h, down_l = halves(grad * slopes[index])
         downs.append((down_h, down_l))
         both = dot(k_tall, jnp.concatenate([down_h, down_l], axis=1))
@@ -444,11 +436,8 @@
             at = slice(256 * d, 256 * d + 256)
             parts.append(both[at, :128] + both[at, 128:] + rest[256 * d - 256 : 256 * d])
         dv_h, dv_l = halves(jnp.concatenate(parts, axis=1))
-        grad = grad + dot(
-            jnp.concatenate([dv_h, dv_l, dv_h], axis=1),
-            jnp.concatenate([high, high, low], axis=1),
-            (1, 1),
-        )
+        both = dot(jnp.concatenate([dv_h, dv_l], axis=1), backward, (1, 1))
+        grad = grad + (both[:, :128] + both[:, 128:])
     (d2_h, d2_l), (d1_h, d1_l) = downs
     (v1_h, v1_l), (v2_h, v2_l) = values
     outer_left = jnp.concatenate([d1_h, d2_h, d1_l, d2_l, d1_h, d2_h], axis=1)
@@ -496,14 +485,14 @@
         return (ox + 2) * n_gy + oy % n_gy
 
     second = []
-    for mx in (-2, 2, -1, 1, 0):
+    for mx in (2, 1, -2, -1, 0):
         for my in (2, -1, 1, 0):
             if (mx, my) != (0, 0):
                 slot = seat(-mx, -my)
                 pair = (send_c, recv_c.at[slot])
                 if abs(mx) == 2:
                     pair = (send_c.at[1], recv_c.at[slot, 1])
-                c = copy(2, *pair, slot, slot, place(mx, my))
+                c = copy(2, *pair, place(mx, my))
                 second.append(c)
                 if mx == -2:
                     pl.when(row != 1)(c.start)
@@ -513,11 +502,10 @@
     @pl.when(row == 1)
     def _():
         pl.semaphore_wait(known_sem, 2)
-        for c in second[:n_gy]:
+        for c in second[2 * n_gy : 3 * n_gy]:
             c.start()
 
-    for c in leave:
-        c.wait_recv()
+    all_of(1, recv_m, 8).wait_recv()
     arriving = jnp.zeros((8, 128), F32)
     for c, m in enumerate(MOVES):
         arriving = jnp.where(rows == c, recv_m[cell(*m)], arriving)
@@ -545,8 +533,7 @@
         hot_spots.append(hit.astype(F32).astype(BF16))
     hot_spots = jnp.concatenate(hot_spots, axis=1)
 
-    for c in second:
-        c.wait_recv()
+    all_of(2, recv_c, 5 * n_gy - 5).wait_recv()
 
     def part(ox, oy, tile):
         if (ox, oy) == (0, 0):
@@ -595,13 +582,13 @@
             ],
             axis=0,
         )
-    for c in first + leave + second:
-        c.wait_send()
+    all_of(0, recv_a, 8).wait_send()
+    all_of(1, recv_m, 8).wait_send()
+    all_of(2, recv_c, 5 * n_gy - 5).wait_send()
 
     @pl.when(row == RELAY)
     def _():
-        for c in relays:
-            c.wait_send()
+        all_of(3, recv_a, 3).wait_send()
 
 
 def store(*refs):
@@ -644,8 +631,8 @@
                 pltpu.VMEM((2, 8, 128), F32),
                 pltpu.VMEM((5 * n_gy, 2, 8, 128), F32),
                 pltpu.SemaphoreType.DMA((len(args),)),
-                pltpu.SemaphoreType.DMA((3, 5 * n_gy)),
-                pltpu.SemaphoreType.DMA((3, 5 * n_gy)),
+                pltpu.SemaphoreType.DMA((4,)),
+                pltpu.SemaphoreType.DMA((4,)),
                 pltpu.SemaphoreType.REGULAR,
                 pltpu.SemaphoreType.REGULAR,
             ],

time: 34.4 us -> 32.3 us (0.939)
  Pallas kernels: 33 us -> 30.8 us
    pallas_call x1, Pallas kernels: 32.3 us -> 30.2 us  [body(): pl.pallas_call(whole, out_shape=outs, in_specs=[smem if name == 'count' e...]
where the time goes in v4:
time: 32.3 us; the launch traced here: 32.1 us
  Pallas kernels  30.8 us (95%)
  between operations  1.29 us (4%)
    pallas_call x1, Pallas kernels, body(): pl.pallas_call(whole, out_shape=outs, in_specs=[smem if name == 'count' e...  30.2 us

profile of v4, /device:TPU:1, one launch (start us, length us, event | category | flops | bytes accessed | tf_op | source)
XLA Modules:
  0.0 32.1 jit_solution(10360537072895607905)
XLA Ops:
  1.3 30.2 %shard_map.219 = (f32[3,128]{1,0:T(4,128)S(1)}, f32[3,128]{1,0:T(4,128)S(1)}, f32[3,128]{1,0:T(4,128)S(1)}, f32[3,3,64]{2,1,0:T(4,128)S(1)}) custom-call(f32[3,128]{1,0:T(4,128)} %refs_0_.1, f32[3,128]{1,0:T(4,128)} %refs_1_.1, f32[3,128]{1,0:T(4,128)} %refs_2_.1, s32[128]{0:T(128)} %refs_3_.1, f32[5]{0:T(128)} %refs_4_.1, s32[64]{0:T(128)} %refs_5_.1, ...), custom_call_target="tpu_custom_call" | custom-call | tf_op jit(solution)/shard_map/pallas_call | solution.py:620
  31.5 0.6 %shard_map.220 = (f32[3,128]{1,0:T(4,128)}, f32[3,128]{1,0:T(4,128)}, f32[3,128]{1,0:T(4,128)}, f32[3,3,64]{2,1,0:T(4,128)}) custom-call(f32[3,128]{1,0:T(4,128)S(1)} %get-tuple-element.8.refs_0_, f32[3,128]{1,0:T(4,128)S(1)} %get-tuple-element.9.refs_1_, f32[3,128]{1,0:T(4,128)S(1)} %get-tuple-element.10.refs_2_, f32[3,3,64]{2,1,0:T(4,128)S(1)} %get-tuple-element.11.refs_3_), custom_call_target="tpu_custom_call" | custom-call | tf_op jit(solution)/shard_map/pallas_call | solution.py:643

commit v5 on v4

--- a/solution.py
+++ b/solution.py
@@ -181,13 +181,17 @@
     xface2 = jnp.concatenate([xface, xface], axis=1)
     yface = yface_ref[...].reshape(1, 128)
     y_owned = yface < 128
+    blank = jnp.full((1, 32), -1, jnp.int32)
+    lower = jnp.concatenate([xface[:, :32]] * 3 + [blank], axis=1)
+    upper = jnp.concatenate([xface[:, 32:]] * 3 + [blank], axis=1)
+    owned_y = jnp.where(y_owned, yface, -1)
     lists = jnp.concatenate(
         [
             jnp.zeros((4, 128), F32),
             yface.astype(F32),
-            xface2.astype(F32),
-            jnp.where(y_owned, yface, -1).astype(F32),
-            jnp.zeros((1, 128), F32),
+            owned_y.astype(F32),
+            lower.astype(F32),
+            upper.astype(F32),
         ],
         axis=0,
     )
@@ -227,7 +231,10 @@
     out = out - jnp.where(field == 0, dx_col, jnp.where(field == 1, dy_col, 0.0))
     out = jnp.where(valid, out, 0.0)
     send_m[...] = jnp.where(field == 9, slots.astype(F32), out)
-    leave = [copy(1, send_m, recv_m.at[cell(*m)], place(*m)) for m in MOVES]
+    leave = [
+        copy(1, send_m.at[pl.ds(c, 1)], recv_m.at[pl.ds(c, 1)], place(*m))
+        for c, m in enumerate(MOVES)
+    ]
     for m, c in zip(MOVES, leave):
         if m[0] == -1:
             pl.when(row > 0)(c.start)
@@ -246,9 +253,12 @@
     hot_n = (iota((384, 256), 0) == place_n).astype(F32)
     hot_c = (iota((128, 256), 0) == center).astype(F32)
     hot_owned = (hot_n[:128] - hot_c).astype(BF16)
-    hot_ghosts = hot_n[128:].astype(BF16)
-    face_rows = jnp.concatenate([jnp.where(y_owned, yface, -1), xface2], axis=1)
-    hot_f = (iota((128, 256), 0) == face_rows).astype(F32).astype(BF16)
+    hot_y = hot_n[256:].astype(BF16)
+    ghost = place_n - 128
+    in_x = (ghost >= 0) & (ghost < 64)
+    at_x = jnp.where(in_x, jnp.where(ghost < 32, 32, 128) + ghost, -1)
+    face_rows = jnp.concatenate([owned_y, lower, upper], axis=1)
+    hot_f = (iota((128, 384), 0) == face_rows).astype(F32).astype(BF16)
     c_live = center.astype(F32)
     rows_e = iota((8, 256), 0)
     left_c = jnp.where(rows_e == 0, jnp.where(live, c_live, -1.0), jnp.where(rows_e == 1, 1.0, 0.0))
@@ -328,7 +338,8 @@
     via_x = listed >= 128
     far_lane = jnp.where(via_x, ((listed - 128) ^ 32) + jnp.where(low_y, 0, 64), 0)
     ghost_y = jnp.where(via_x, lanes_at(far_x, far_lane), ghost_y) + y_shift
-    ghost_y = jnp.where(rows == 4, jnp.where(via_x, far_lane.astype(F32), -1.0), ghost_y)
+    far_at = (far_lane + 96 * ((far_lane // 32) % 2)).astype(F32)
+    ghost_y = jnp.where(rows == 4, jnp.where(via_x, far_at, -1.0), ghost_y)
 
     def edge_side(tiles, index):
         parts = []
@@ -344,7 +355,8 @@
 
     near = edge_side([record, ghost_x, ghost_y], place_n)
     own = edge_side([record], center)
-    hot_far = (iota((128, 256), 0) == near[4:5].astype(jnp.int32)).astype(F32).astype(BF16)
+    side = iota((256, 256), 0)
+    hot_x = (side == jnp.where(in_x, at_x, near[4:5].astype(jnp.int32))).astype(F32).astype(BF16)
 
     offset = (near - own) * (1.0 / CUTOFF)
     ux, uy, uz = offset[0:1], offset[1:2], offset[2:3]
@@ -469,17 +481,16 @@
     dux = d_tees[0:1] + ux * (d_squared + dxx - dzz) + uy * dxy + uz * dzx
     duy = d_tees[1:2] + uy * (d_squared - dxx - dzz) + ux * dxy + uz * dyz
     duz = d_tees[2:3] + uz * (d_squared + 2.0 * dzz) + uy * dyz + ux * dzx
-    d_edge = jnp.concatenate([dux, duy, duz, dux, duy, duz, jnp.zeros((2, 256), F32)], axis=0)
+    d_edge = jnp.concatenate([dux, duy, duz, jnp.zeros((5, 256), F32)], axis=0)
     d_edge = jnp.where(live, d_edge * (1.0 / CUTOFF), 0.0)
     d_edge_h, d_edge_l = halves_f32(d_edge)
     d_pair = jnp.concatenate([d_edge_h, d_edge_l], axis=0).astype(BF16)
 
-    spread = dot(d_pair, jnp.concatenate([hot_owned, hot_ghosts, hot_far], axis=0), (1, 1))
-    spread = spread[:8] + spread[8:]
-    own_y = jnp.where(rows < 3, spread[:, :128], spread[:, 256:384])
-    far_x = jnp.where(rows < 3, spread[:, 384:], spread[:, 128:256])
-    send_c[0] = own_y
-    send_c[1] = far_x
+    spread = dot(d_pair, jnp.concatenate([hot_owned, hot_y, hot_x], axis=0), (1, 1))
+    spread = spread[:4] + spread[8:12]
+    mine = (spread[:, 384:], spread[:, :128], spread[:, 128:256], spread[:, 256:384])
+    for number, value in enumerate(mine):
+        send_c[number] = value
 
     def seat(ox, oy):
         return (ox + 2) * n_gy + oy % n_gy
@@ -489,10 +500,8 @@
         for my in (2, -1, 1, 0):
             if (mx, my) != (0, 0):
                 slot = seat(-mx, -my)
-                pair = (send_c, recv_c.at[slot])
-                if abs(mx) == 2:
-                    pair = (send_c.at[1], recv_c.at[slot, 1])
-                c = copy(2, *pair, place(mx, my))
+                used = {-2: (0, 1), -1: (0, 3), 0: (0, 4), 1: (1, 3), 2: (3, 1)}[mx]
+                c = copy(2, send_c.at[pl.ds(*used)], recv_c.at[slot, pl.ds(*used)], place(mx, my))
                 second.append(c)
                 if mx == -2:
                     pl.when(row != 1)(c.start)
@@ -506,9 +515,7 @@
             c.start()
 
     all_of(1, recv_m, 8).wait_recv()
-    arriving = jnp.zeros((8, 128), F32)
-    for c, m in enumerate(MOVES):
-        arriving = jnp.where(rows == c, recv_m[cell(*m)], arriving)
+    arriving = recv_m[...]
     slot_lane = lane % 8
     gains = lanes_at(arriving, 64 + slot_lane)
     listed = lanes_at(arriving, 72 + slot_lane)
@@ -524,44 +531,44 @@
         axis=1,
         keepdims=True,
     )
-    spot_source = iota((64, 256), 0) // 8
+    spot_source = iota((64, 384), 0) // 8
     hot_spots = []
     for c, m in enumerate(MOVES):
         tile = recv_a[cell(*m)]
-        faces = jnp.concatenate([tile[6:7], tile[5:6]], axis=1)
+        faces = jnp.concatenate([tile[5:6], tile[6:7], tile[7:8]], axis=1)
         hit = jnp.where(spot_source == c, faces, -2.0) == listed_col
         hot_spots.append(hit.astype(F32).astype(BF16))
     hot_spots = jnp.concatenate(hot_spots, axis=1)
 
-    all_of(2, recv_c, 5 * n_gy - 5).wait_recv()
+    all_of(2, recv_c, 3 * n_gy - 1).wait_recv()
 
     def part(ox, oy, tile):
         if (ox, oy) == (0, 0):
-            return (own_y, far_x)[tile]
+            return mine[tile]
         return recv_c[seat(ox, oy), tile]
 
+    third = lane // 32
+
     def inward(bx, by):
-        from_y = jnp.where(low_y, part(bx, by - 1, 0), part(bx, by + 1, 0))
-        from_x = jnp.where(low_x, part(bx - 1, by, 1), part(bx + 1, by, 1))
-        from_far = pick4(
-            [part(bx + sx, by + sy, 1) for sx, sy in ((-1, -1), (1, -1), (-1, 1), (1, 1))]
-        )
-        both = jnp.concatenate(
-            [jnp.where(rows < 3, 0.0, from_y), jnp.where(rows < 3, from_far, from_x)], axis=1
-        )
-        return jnp.concatenate(halves_f32(both), axis=0).astype(BF16)
+        sides = [jnp.where(low_y, part(bx, by - 1, 2), part(bx, by + 1, 2))]
+        for ox, tile in ((bx - 1, 3), (bx + 1, 0)):
+            above, beside = part(ox, by - 1, tile), part(ox, by, tile)
+            below = part(ox, by + 1, tile)
+            sides.append(jnp.where(third == 0, above, jnp.where(third == 1, beside, below)))
+        high, low = halves_f32(jnp.concatenate(sides, axis=1))
+        return jnp.concatenate([high, low, jnp.zeros((8, 384), F32)], axis=0).astype(BF16)
 
     def force_of(owned, back):
-        back = back[:8] + back[8:]
-        return -(owned[:3] + back[:3] + back[3:6])
-
-    force = force_of(own_y, dot(inward(0, 0), hot_f, (1, 1)))
+        return -(owned[:3] + back[:3] + back[4:7])
+
+    force = force_of(mine[1], dot(inward(0, 0), hot_f, (1, 1)))
     new_frc_ref[...] = force
     new_vel_ref[...] = halfway + gain * force
 
     owned = jnp.zeros((8, 128), F32)
     for c, m in enumerate(MOVES):
-        owned = jnp.where(field == c, lanes_at(part(-m[0], -m[1], 0), listed_at), owned)
+        tile = jnp.concatenate([part(-m[0], -m[1], 1)] * 2, axis=0)
+        owned = jnp.where(field == c, lanes_at(tile, listed_at), owned)
     back = dot(
         jnp.concatenate([inward(-m[0], -m[1]) for m in MOVES], axis=1), hot_spots, (1, 1)
     )
@@ -584,7 +591,7 @@
         )
     all_of(0, recv_a, 8).wait_send()
     all_of(1, recv_m, 8).wait_send()
-    all_of(2, recv_c, 5 * n_gy - 5).wait_send()
+    all_of(2, recv_c, 3 * n_gy - 1).wait_send()
 
     @pl.when(row == RELAY)
     def _():
@@ -615,7 +622,6 @@
         atoms = jax.ShapeDtypeStruct(args[0].shape, F32)
         outs = (atoms, atoms, atoms, jax.ShapeDtypeStruct((3, 3, 64), F32))
         tile = pltpu.VMEM((8, 128), F32)
-        tiles = pltpu.VMEM((9, 8, 128), F32)
         scalars = ("inv_mass", "count")
         results = pl.pallas_call(
             whole,
@@ -626,10 +632,10 @@
                 (pltpu.SMEM if name in scalars else pltpu.VMEM)(arg.shape, arg.dtype)
                 for name, arg in zip(INPUTS, args)
             ]
-            + [tile, tile, pltpu.VMEM((12, 8, 128), F32), tile, tiles]
+            + [tile, tile, pltpu.VMEM((12, 8, 128), F32), tile, tile]
             + [
-                pltpu.VMEM((2, 8, 128), F32),
-                pltpu.VMEM((5 * n_gy, 2, 8, 128), F32),
+                pltpu.VMEM((4, 4, 128), F32),
+                pltpu.VMEM((5 * n_gy, 4, 4, 128), F32),
                 pltpu.SemaphoreType.DMA((len(args),)),
                 pltpu.SemaphoreType.DMA((4,)),
                 pltpu.SemaphoreType.DMA((4,)),

time: 32.3 us -> 32 us (level)
  no operation moved by 1% of the time
where the time goes in v5:
time: 32 us; the launch traced here: 31.9 us
  Pallas kernels  30.6 us (96%)
  between operations  1.29 us (4%)
    pallas_call x1, Pallas kernels, body(): pl.pallas_call(whole, out_shape=outs, in_specs=[smem if name == 'count' e...  29.9 us
    pallas_call x1, Pallas kernels, body(): pl.pallas_call(store, out_shape=outs, in_specs=[vmem] * 4, out_specs=(hbm...  0.64 us

profile of v5, /device:TPU:1, one launch (start us, length us, event | category | flops | bytes accessed | tf_op | source)
XLA Modules:
  0.0 31.9 jit_solution(18170322543766490729)
XLA Ops:
  1.3 29.9 %shard_map.219 = (f32[3,128]{1,0:T(4,128)S(1)}, f32[3,128]{1,0:T(4,128)S(1)}, f32[3,128]{1,0:T(4,128)S(1)}, f32[3,3,64]{2,1,0:T(4,128)S(1)}) custom-call(f32[3,128]{1,0:T(4,128)} %refs_0_.1, f32[3,128]{1,0:T(4,128)} %refs_1_.1, f32[3,128]{1,0:T(4,128)} %refs_2_.1, s32[128]{0:T(128)} %refs_3_.1, f32[5]{0:T(128)} %refs_4_.1, s32[64]{0:T(128)} %refs_5_.1, ...), custom_call_target="tpu_custom_call" | custom-call | tf_op jit(solution)/shard_map/pallas_call | solution.py:626
  31.2 0.6 %shard_map.220 = (f32[3,128]{1,0:T(4,128)}, f32[3,128]{1,0:T(4,128)}, f32[3,128]{1,0:T(4,128)}, f32[3,3,64]{2,1,0:T(4,128)}) custom-call(f32[3,128]{1,0:T(4,128)S(1)} %get-tuple-element.8.refs_0_, f32[3,128]{1,0:T(4,128)S(1)} %get-tuple-element.9.refs_1_, f32[3,128]{1,0:T(4,128)S(1)} %get-tuple-element.10.refs_2_, f32[3,3,64]{2,1,0:T(4,128)S(1)} %get-tuple-element.11.refs_3_), custom_call_target="tpu_custom_call" | custom-call | tf_op jit(solution)/shard_map/pallas_call | solution.py:649

commit v6 on v5

--- a/solution.py
+++ b/solution.py
@@ -250,6 +250,14 @@
         neighbor,
         jnp.where(neighbor < 192, ((neighbor - 128) ^ 32) + 128, ((neighbor - 192) ^ 64) + 256),
     )
+
+    def edge_side(tile, index):
+        return jnp.concatenate(
+            [lanes_at(tile, index[:, 128 * h : 128 * h + 128] & 127) for h in range(2)], axis=1
+        )
+
+    own = edge_side(record, center)
+    near_owned = edge_side(record, place_n)
     hot_n = (iota((384, 256), 0) == place_n).astype(F32)
     hot_c = (iota((128, 256), 0) == center).astype(F32)
     hot_owned = (hot_n[:128] - hot_c).astype(BF16)
@@ -284,7 +292,11 @@
                 axis=1,
             )
         )
-        return doubled(high, low)
+        blocks = [
+            doubled(high[:, 128 * d : 128 * d + 128], low[:, 128 * d : 128 * d + 128])
+            for d in range(3)
+        ]
+        return tuple(jnp.concatenate(each, axis=1) for each in zip(*blocks))
 
     tensor1_ref, mix1_ref, tensor2_ref, mix2_ref = loaded("tensor1", "mix1", "tensor2", "mix2")
     final_ref, radial_ref, emb_c_ref, emb_n_ref = loaded("final", "radial", "emb_c", "emb_n")
@@ -341,20 +353,11 @@
     far_at = (far_lane + 96 * ((far_lane // 32) % 2)).astype(F32)
     ghost_y = jnp.where(rows == 4, jnp.where(via_x, far_at, -1.0), ghost_y)
 
-    def edge_side(tiles, index):
-        parts = []
-        for half in range(2):
-            at = index[:, 128 * half : 128 * half + 128]
-            result = lanes_at(tiles[0], at & 127)
-            for number in range(1, len(tiles)):
-                result = jnp.where(
-                    at >= 128 * number, lanes_at(tiles[number], at & 127), result
-                )
-            parts.append(result)
-        return jnp.concatenate(parts, axis=1)
-
-    near = edge_side([record, ghost_x, ghost_y], place_n)
-    own = edge_side([record], center)
+    near = jnp.where(
+        place_n < 128,
+        near_owned,
+        jnp.where(place_n < 256, edge_side(ghost_x, place_n), edge_side(ghost_y, place_n)),
+    )
     side = iota((256, 256), 0)
     hot_x = (side == jnp.where(in_x, at_x, near[4:5].astype(jnp.int32))).astype(F32).astype(BF16)
 
@@ -409,20 +412,13 @@
     for forward, _ in layers:
         hid_h, hid_l = halves(hidden)
         pair = dot(jnp.concatenate([hid_h, hid_l], axis=1), forward)
-        value = pair[:, :384] + pair[:, 384:]
-        val_h, val_l = halves(value)
-        values.append((val_h, val_l))
-        both = dot(
-            k_wide,
-            jnp.concatenate(
-                [
-                    jnp.concatenate([val_h[:, 128 * d : 128 * d + 128], val_l[:, 128 * d : 128 * d + 128]], axis=1)
-                    for d in range(3)
-                ],
-                axis=0,
-            ),
-        )
-        rest = dot(k_wide_l, jnp.concatenate([val_h[:, 128:256], val_h[:, 256:384]], axis=0))
+        split = [
+            halves(pair[:, 256 * d : 256 * d + 128] + pair[:, 256 * d + 128 : 256 * d + 256])
+            for d in range(3)
+        ]
+        values.append(split)
+        both = sum(dot(k, jnp.concatenate(split[d], axis=1)) for d, k in enumerate((k0, k1_h, k2_h)))
+        rest = dot(k1_l, split[1][0]) + dot(k2_l, split[2][0])
         pre = both[:, :128] + both[:, 128:] + rest
         sig = sigmoid(pre)
         hidden = hidden + pre * sig
@@ -447,29 +443,26 @@
         for d in (1, 2):
             at = slice(256 * d, 256 * d + 256)
             parts.append(both[at, :128] + both[at, 128:] + rest[256 * d - 256 : 256 * d])
-        dv_h, dv_l = halves(jnp.concatenate(parts, axis=1))
-        both = dot(jnp.concatenate([dv_h, dv_l], axis=1), backward, (1, 1))
+        both = dot(
+            jnp.concatenate([half for part in parts for half in halves(part)], axis=1),
+            backward,
+            (1, 1),
+        )
         grad = grad + (both[:, :128] + both[:, 128:])
     (d2_h, d2_l), (d1_h, d1_l) = downs
-    (v1_h, v1_l), (v2_h, v2_l) = values
     outer_left = jnp.concatenate([d1_h, d2_h, d1_l, d2_l, d1_h, d2_h], axis=1)
     moved = []
     for d in (1, 2):
-        at = slice(128 * d, 128 * d + 128)
+        (v1_h, v1_l), (v2_h, v2_l) = values[0][d], values[1][d]
         outer = dot(
-            outer_left,
-            jnp.concatenate(
-                [v1_h[:, at], v2_h[:, at], v1_h[:, at], v2_h[:, at], v1_l[:, at], v2_l[:, at]],
-                axis=1,
-            ),
-            (1, 1),
+            outer_left, jnp.concatenate([v1_h, v2_h, v1_h, v2_h, v1_l, v2_l], axis=1), (1, 1)
         )
-        out_h, out_l = halves(jnp.where(same, outer, 0.0))
+        turned = jnp.where(same, outer, 0.0)
+        out_h, out_l = halves(turned + turned.T)
         pair = jnp.concatenate([tees_h, tees_l], axis=0).astype(BF16)
         high_t = tees_h.astype(BF16)
-        first_part = dot(pair, out_h) + dot(pair, out_h, (1, 1))
-        second_part = dot(high_t, out_l) + dot(high_t, out_l, (1, 1))
-        moved.append(first_part[:8] + first_part[8:] + second_part)
+        first_part = dot(pair, out_h)
+        moved.append(first_part[:8] + first_part[8:] + dot(high_t, out_l))
     d_tees = jnp.where(rows_e < 3, moved[0], moved[1])
 
     g_h, g_l = halves(grad * slope0)

time: 32 us -> 31.8 us (level)
  no operation moved by 1% of the time
where the time goes in v6:
time: 31.8 us; the launch traced here: 31.6 us
  Pallas kernels  30.3 us (95%)
  between operations  1.29 us (4%)
    pallas_call x1, Pallas kernels, body(): pl.pallas_call(whole, out_shape=outs, in_specs=[smem if name == 'count' e...  29.7 us
    pallas_call x1, Pallas kernels, body(): pl.pallas_call(store, out_shape=outs, in_specs=[vmem] * 4, out_specs=(hbm...  0.64 us

profile of v6, /device:TPU:1, one launch (start us, length us, event | category | flops | bytes accessed | tf_op | source)
XLA Modules:
  0.0 31.6 jit_solution(2621812242091631206)
XLA Ops:
  1.3 29.7 %shard_map.219 = (f32[3,128]{1,0:T(4,128)S(1)}, f32[3,128]{1,0:T(4,128)S(1)}, f32[3,128]{1,0:T(4,128)S(1)}, f32[3,3,64]{2,1,0:T(4,128)S(1)}) custom-call(f32[3,128]{1,0:T(4,128)} %refs_0_.1, f32[3,128]{1,0:T(4,128)} %refs_1_.1, f32[3,128]{1,0:T(4,128)} %refs_2_.1, s32[128]{0:T(128)} %refs_3_.1, f32[5]{0:T(128)} %refs_4_.1, s32[64]{0:T(128)} %refs_5_.1, ...), custom_call_target="tpu_custom_call" | custom-call | tf_op jit(solution)/shard_map/pallas_call | solution.py:619
  31.0 0.6 %shard_map.220 = (f32[3,128]{1,0:T(4,128)}, f32[3,128]{1,0:T(4,128)}, f32[3,128]{1,0:T(4,128)}, f32[3,3,64]{2,1,0:T(4,128)}) custom-call(f32[3,128]{1,0:T(4,128)S(1)} %get-tuple-element.8.refs_0_, f32[3,128]{1,0:T(4,128)S(1)} %get-tuple-element.9.refs_1_, f32[3,128]{1,0:T(4,128)S(1)} %get-tuple-element.10.refs_2_, f32[3,3,64]{2,1,0:T(4,128)S(1)} %get-tuple-element.11.refs_3_), custom_call_target="tpu_custom_call" | custom-call | tf_op jit(solution)/shard_map/pallas_call | solution.py:642

commit v7 on v6

--- a/solution.py
+++ b/solution.py
@@ -18,7 +18,7 @@
 MOVES = tuple((a, b) for a in (-1, 0, 1) for b in (-1, 0, 1) if (a, b) != (0, 0))
 ROW = 32
 RELAY = 3
-FAR_FIRST = tuple(sorted(MOVES, key=lambda move: -abs(move[0])))
+FAR_FIRST = tuple(sorted(MOVES, key=lambda move: (-abs(move[0]), -move[0])))
 
 
 INPUTS = (
@@ -108,8 +108,13 @@
     gy = lax.axis_index("gy")
     row = lax.rem(gx, ROW)
 
+    near_x = {dx: lax.rem(gx + (dx + n_gx), n_gx) for dx in (-2, -1, 0, 1, 2)}
+    near_y = {dy: lax.rem(gy + (dy + n_gy), n_gy) for dy in (-1, 0, 1, 2)}
+
     def place(dx, dy):
-        return (lax.rem(gx + (dx + n_gx), n_gx), lax.rem(gy + (dy + n_gy), n_gy))
+        if isinstance(dx, int) and dx in near_x:
+            return near_x[dx], near_y[dy]
+        return lax.rem(gx + (dx + n_gx), n_gx), near_y[dy]
 
     def signal(semaphore, target):
         pl.semaphore_signal(semaphore, inc=1, device_id=target, device_id_type=MESH)
@@ -235,10 +240,14 @@
         copy(1, send_m.at[pl.ds(c, 1)], recv_m.at[pl.ds(c, 1)], place(*m))
         for c, m in enumerate(MOVES)
     ]
+    leave_back = [c for m, c in zip(MOVES, leave) if m[0] == -1]
     for m, c in zip(MOVES, leave):
-        if m[0] == -1:
-            pl.when(row > 0)(c.start)
-        else:
+        if m[0] != -1:
+            c.start()
+
+    @pl.when(row > 0)
+    def _():
+        for c in leave_back:
             c.start()
 
     neighbor_ref, center_ref = loaded("neighbor", "center")
@@ -325,9 +334,8 @@
     def _():
         signal(known_sem, place(1, 0))
         signal(known_sem, place(1, 1))
-        for m, c in zip(MOVES, leave):
-            if m[0] == -1:
-                c.start()
+        for c in leave_back:
+            c.start()
 
     def pick4(tiles):
         quarter = lane // 32
@@ -411,11 +419,11 @@
     slopes, values = [], []
     for forward, _ in layers:
         hid_h, hid_l = halves(hidden)
-        pair = dot(jnp.concatenate([hid_h, hid_l], axis=1), forward)
-        split = [
-            halves(pair[:, 256 * d : 256 * d + 128] + pair[:, 256 * d + 128 : 256 * d + 256])
-            for d in range(3)
-        ]
+        hid = jnp.concatenate([hid_h, hid_l], axis=1)
+        split = []
+        for d in range(3):
+            pair = dot(hid, forward[:, 256 * d : 256 * d + 256])
+            split.append(halves(pair[:, :128] + pair[:, 128:]))
         values.append(split)
         both = sum(dot(k, jnp.concatenate(split[d], axis=1)) for d, k in enumerate((k0, k1_h, k2_h)))
         rest = dot(k1_l, split[1][0]) + dot(k2_l, split[2][0])
@@ -488,23 +496,28 @@
     def seat(ox, oy):
         return (ox + 2) * n_gy + oy % n_gy
 
-    second = []
-    for mx in (2, 1, -2, -1, 0):
-        for my in (2, -1, 1, 0):
-            if (mx, my) != (0, 0):
-                slot = seat(-mx, -my)
-                used = {-2: (0, 1), -1: (0, 3), 0: (0, 4), 1: (1, 3), 2: (3, 1)}[mx]
-                c = copy(2, send_c.at[pl.ds(*used)], recv_c.at[slot, pl.ds(*used)], place(mx, my))
-                second.append(c)
-                if mx == -2:
-                    pl.when(row != 1)(c.start)
-                else:
-                    c.start()
+    second = {}
+    for mx, used in ((2, (3, 1)), (1, (1, 3)), (-2, (0, 1)), (-1, (0, 3)), (0, (0, 4))):
+        second[mx] = [
+            copy(2, send_c.at[pl.ds(*used)], recv_c.at[seat(-mx, -my), pl.ds(*used)], place(mx, my))
+            for my in (2, -1, 1, 0)
+            if (mx, my) != (0, 0)
+        ]
+    for c in second[2] + second[1]:
+        c.start()
+
+    @pl.when(row != 1)
+    def _():
+        for c in second[-2]:
+            c.start()
+
+    for c in second[-1] + second[0]:
+        c.start()
 
     @pl.when(row == 1)
     def _():
         pl.semaphore_wait(known_sem, 2)
-        for c in second[2 * n_gy : 3 * n_gy]:
+        for c in second[-2]:
             c.start()
 
     all_of(1, recv_m, 8).wait_recv()
@@ -533,6 +546,14 @@
         hot_spots.append(hit.astype(F32).astype(BF16))
     hot_spots = jnp.concatenate(hot_spots, axis=1)
 
+    all_of(0, recv_a, 8).wait_send()
+    all_of(1, recv_m, 8).wait_send()
+
+    @pl.when(row == RELAY)
+    def _():
+        all_of(3, recv_a, 3).wait_send()
+
+    all_of(2, recv_c, 3 * n_gy - 1).wait_send()
     all_of(2, recv_c, 3 * n_gy - 1).wait_recv()
 
     def part(ox, oy, tile):
@@ -582,13 +603,6 @@
             ],
             axis=0,
         )
-    all_of(0, recv_a, 8).wait_send()
-    all_of(1, recv_m, 8).wait_send()
-    all_of(2, recv_c, 3 * n_gy - 1).wait_send()
-
-    @pl.when(row == RELAY)
-    def _():
-        all_of(3, recv_a, 3).wait_send()
 
 
 def store(*refs):

time: 31.8 us -> 31.7 us (level)
  no operation moved by 1% of the time
where the time goes in v7:
time: 31.7 us; the launch traced here: 31.5 us
  Pallas kernels  30.2 us (95%)
  between operations  1.29 us (4%)
    pallas_call x1, Pallas kernels, body(): pl.pallas_call(whole, out_shape=outs, in_specs=[smem if name == 'count' e...  29.6 us
    pallas_call x1, Pallas kernels, body(): pl.pallas_call(store, out_shape=outs, in_specs=[vmem] * 4, out_specs=(hbm...  0.64 us

profile of v7, /device:TPU:1, one launch (start us, length us, event | category | flops | bytes accessed | tf_op | source)
XLA Modules:
  0.0 31.5 jit_solution(622719493556346766)
XLA Ops:
  1.3 29.6 %shard_map.219 = (f32[3,128]{1,0:T(4,128)S(1)}, f32[3,128]{1,0:T(4,128)S(1)}, f32[3,128]{1,0:T(4,128)S(1)}, f32[3,3,64]{2,1,0:T(4,128)S(1)}) custom-call(f32[3,128]{1,0:T(4,128)} %refs_0_.1, f32[3,128]{1,0:T(4,128)} %refs_1_.1, f32[3,128]{1,0:T(4,128)} %refs_2_.1, s32[128]{0:T(128)} %refs_3_.1, f32[5]{0:T(128)} %refs_4_.1, s32[64]{0:T(128)} %refs_5_.1, ...), custom_call_target="tpu_custom_call" | custom-call | tf_op jit(solution)/shard_map/pallas_call | solution.py:633
  30.9 0.6 %shard_map.220 = (f32[3,128]{1,0:T(4,128)}, f32[3,128]{1,0:T(4,128)}, f32[3,128]{1,0:T(4,128)}, f32[3,3,64]{2,1,0:T(4,128)}) custom-call(f32[3,128]{1,0:T(4,128)S(1)} %get-tuple-element.8.refs_0_, f32[3,128]{1,0:T(4,128)S(1)} %get-tuple-element.9.refs_1_, f32[3,128]{1,0:T(4,128)S(1)} %get-tuple-element.10.refs_2_, f32[3,3,64]{2,1,0:T(4,128)S(1)} %get-tuple-element.11.refs_3_), custom_call_target="tpu_custom_call" | custom-call | tf_op jit(solution)/shard_map/pallas_call | solution.py:656

commit v8 on v6

--- a/solution.py
+++ b/solution.py
@@ -411,11 +411,11 @@
     slopes, values = [], []
     for forward, _ in layers:
         hid_h, hid_l = halves(hidden)
-        pair = dot(jnp.concatenate([hid_h, hid_l], axis=1), forward)
-        split = [
-            halves(pair[:, 256 * d : 256 * d + 128] + pair[:, 256 * d + 128 : 256 * d + 256])
-            for d in range(3)
-        ]
+        hid = jnp.concatenate([hid_h, hid_l], axis=1)
+        split = []
+        for d in range(3):
+            pair = dot(hid, forward[:, 256 * d : 256 * d + 256])
+            split.append(halves(pair[:, :128] + pair[:, 128:]))
         values.append(split)
         both = sum(dot(k, jnp.concatenate(split[d], axis=1)) for d, k in enumerate((k0, k1_h, k2_h)))
         rest = dot(k1_l, split[1][0]) + dot(k2_l, split[2][0])
@@ -454,8 +454,10 @@
     moved = []
     for d in (1, 2):
         (v1_h, v1_l), (v2_h, v2_l) = values[0][d], values[1][d]
-        outer = dot(
-            outer_left, jnp.concatenate([v1_h, v2_h, v1_h, v2_h, v1_l, v2_l], axis=1), (1, 1)
+        outer = (
+            dot(jnp.concatenate([d2_h, d2_l], axis=1), jnp.concatenate([v2_h, v2_h], axis=1), (1, 1))
+            + dot(jnp.concatenate([d1_h, d1_l], axis=1), jnp.concatenate([v1_h, v1_h], axis=1), (1, 1))
+            + dot(jnp.concatenate([d1_h, d2_h], axis=1), jnp.concatenate([v1_l, v2_l], axis=1), (1, 1))
         )
         turned = jnp.where(same, outer, 0.0)
         out_h, out_l = halves(turned + turned.T)

time: 31.8 us -> 31.8 us (level)
  no operation moved by 1% of the time
where the time goes in v8:
time: 31.8 us; the launch traced here: 31.6 us
  Pallas kernels  30.3 us (95%)
  between operations  1.29 us (4%)
    pallas_call x1, Pallas kernels, body(): pl.pallas_call(whole, out_shape=outs, in_specs=[smem if name == 'count' e...  29.7 us
    pallas_call x1, Pallas kernels, body(): pl.pallas_call(store, out_shape=outs, in_specs=[vmem] * 4, out_specs=(hbm...  0.64 us

profile of v8, /device:TPU:1, one launch (start us, length us, event | category | flops | bytes accessed | tf_op | source)
XLA Modules:
  0.0 31.6 jit_solution(15473123900312542567)
XLA Ops:
  1.3 29.7 %shard_map.219 = (f32[3,128]{1,0:T(4,128)S(1)}, f32[3,128]{1,0:T(4,128)S(1)}, f32[3,128]{1,0:T(4,128)S(1)}, f32[3,3,64]{2,1,0:T(4,128)S(1)}) custom-call(f32[3,128]{1,0:T(4,128)} %refs_0_.1, f32[3,128]{1,0:T(4,128)} %refs_1_.1, f32[3,128]{1,0:T(4,128)} %refs_2_.1, s32[128]{0:T(128)} %refs_3_.1, f32[5]{0:T(128)} %refs_4_.1, s32[64]{0:T(128)} %refs_5_.1, ...), custom_call_target="tpu_custom_call" | custom-call | tf_op jit(solution)/shard_map/pallas_call | solution.py:621
  31.0 0.6 %shard_map.220 = (f32[3,128]{1,0:T(4,128)}, f32[3,128]{1,0:T(4,128)}, f32[3,128]{1,0:T(4,128)}, f32[3,3,64]{2,1,0:T(4,128)}) custom-call(f32[3,128]{1,0:T(4,128)S(1)} %get-tuple-element.8.refs_0_, f32[3,128]{1,0:T(4,128)S(1)} %get-tuple-element.9.refs_1_, f32[3,128]{1,0:T(4,128)S(1)} %get-tuple-element.10.refs_2_, f32[3,3,64]{2,1,0:T(4,128)S(1)} %get-tuple-element.11.refs_3_), custom_call_target="tpu_custom_call" | custom-call | tf_op jit(solution)/shard_map/pallas_call | solution.py:644
